TPU v7x, 512 devices: a whole 4x8x8 slice. The times are simulated.
512 devices in a mesh: fsdp: 16 (over z, y_lo), ctx: 32 (over y_hi, x, core).
Axes of the slice: x: 4, y: 8 (y_hi: 4, y_lo: 2; y = y_hi * 2 + y_lo), z: 8, core: 2. Of those that a mesh axis runs over, the one named last changes fastest.
Arguments:
- hidden: bfloat16 [16, 4096, 8192], P('fsdp', 'ctx'), may hold values from -6 to 6
- values: bfloat16 [16, 4096, 4096], P('fsdp', 'ctx'), may hold values from -6 to 6
- targets: bfloat16 [16, 4096, 4096], P('fsdp', 'ctx'), may hold values from -6 to 6
- dt_raw: float32 [16, 32, 4096], P('fsdp', None, 'ctx'), as said below
- proj_weight: bfloat16 [8192, 128], P('fsdp'), may hold values from -0.0234375 to 0.0234375
- a_log: float32 [32], replicated
- skip: float32 [32], replicated, may hold values from 0.5 to 1.5
Outputs:
- grad_w: float32 [8192, 128], P('fsdp')
- grad_a_log: float32 [32], replicated
- grad_skip: float32 [32], replicated
- loss: float32 [], replicated
Inputs may be any that keep to these rules, and one draw needn't show every extreme that they name: softplus(dt_raw) is the step size of a head at a position.
All inputs are finite; a program needn't handle non-finite values.
Results may differ from a plain program's by a relative error of at most 0.004.
Values may be sent and summed in bfloat16 or wider, within the bound.
A program may use at most 192 MiB of HBM per device.

v0:
```python
import math

import jax
import jax.numpy as jnp
from jax import lax
from jax.sharding import PartitionSpec as P

highest = lax.Precision.HIGHEST


def prefix(value, axis, join, neutral, backward):
    count, mine = (lax.axis_size(axis), lax.axis_index(axis))
    pieces = jax.tree.map(lambda part: lax.all_gather(part, axis), value)
    if backward:
        pieces = jax.tree.map(lambda part: part[::-1], pieces)
        mine = count - 1 - mine
    subtotal = jax.tree.map(
        lambda part, zero: jnp.full_like(part, 0) + jnp.asarray(zero, part.dtype), value, neutral
    )

    def hop(position, subtotal):
        longer = join(subtotal, jax.tree.map(lambda part: part[position], pieces))
        return jax.tree.map(lambda new, old: jnp.where(position < mine, new, old), longer, subtotal)

    return lax.fori_loop(0, count - 1, hop, subtotal)


def product(form, left, right):
    return jnp.einsum(form, left, right, preferred_element_type=jnp.float32)


def block_local(proj, step_size, decay_rate, vals, lower_mask):
    row_count = proj.shape[0]
    head_count = step_size.shape[0]
    state_width = proj.shape[1] // 2
    input_map = proj[:, :state_width]
    output_map = proj[:, state_width:]
    decay_sum = jnp.cumsum(step_size * decay_rate[:, None], axis=1)
    final = decay_sum[:, -1:]
    scores = jnp.dot(output_map, input_map.T, preferred_element_type=jnp.float32)
    within = jnp.where(
        lower_mask[None] > 0,
        jnp.exp(jnp.minimum(decay_sum[:, :, None] - decay_sum[:, None, :], 0.0)),
        0.0,
    )
    mixing = within * scores[None] * step_size[:, None, :]
    inputs = vals.reshape(row_count, head_count, vals.shape[1] // head_count)
    inner_out = product("hts,shp->thp", mixing.astype(jnp.bfloat16), inputs)
    to_end = jnp.exp(final - decay_sum)
    weight_end = to_end * step_size
    coef = (weight_end[:, None, :] * input_map.T.astype(jnp.float32)[None]).astype(jnp.bfloat16)
    local_state = product("hns,shp->hnp", coef, inputs)
    growth = jnp.exp(decay_sum)
    carry = jnp.exp(final[:, 0])
    return (
        input_map,
        output_map,
        step_size,
        decay_sum,
        within,
        mixing,
        inputs,
        to_end,
        weight_end,
        growth,
        local_state,
        carry,
        inner_out,
    )


def block_output(pack, state_in, wanted, skip_gain):
    (
        input_map,
        output_map,
        step_size,
        decay_sum,
        within,
        mixing,
        inputs,
        to_end,
        weight_end,
        growth,
        local_state,
        carry,
        inner_out,
    ) = pack
    state_bf = state_in.astype(jnp.bfloat16)
    from_state = product("hnp,tn->thp", state_bf, output_map)
    outputs = (
        inner_out
        + growth.T[:, :, None] * from_state
        + skip_gain[None, :, None] * inputs.astype(jnp.float32)
    )
    misfit = outputs - wanted.reshape(inputs.shape).astype(jnp.float32)
    return (misfit, from_state, state_bf)


def block_return(pack, from_state, state_bf, misfit, loss_scale):
    (
        input_map,
        output_map,
        step_size,
        decay_sum,
        within,
        mixing,
        inputs,
        to_end,
        weight_end,
        growth,
        local_state,
        carry,
        inner_out,
    ) = pack
    grad_out = misfit * loss_scale
    skip_part = jnp.sum(grad_out * inputs.astype(jnp.float32), axis=(0, 2))
    grad_bf = grad_out.astype(jnp.bfloat16)
    mix_grad = product("thp,shp->hts", grad_bf, inputs)
    score_grad = jnp.sum(within * mix_grad * step_size[:, None, :], axis=0)
    weighted = mix_grad * mixing
    sum_grad = (
        jnp.sum(weighted, axis=2)
        - jnp.sum(weighted, axis=1)
        + growth * jnp.sum(grad_out * from_state, axis=2).T
    )
    grown_bf = (growth.T[:, :, None] * grad_out).astype(jnp.bfloat16)
    entry_grad = product("thp,tn->hnp", grown_bf, output_map)
    score_bf = score_grad.astype(jnp.bfloat16)
    out_grad = product("thp,hnp->tn", grown_bf, state_bf) + product(
        "ts,sn->tn", score_bf, input_map
    )
    in_grad = product("ts,tn->sn", score_bf, output_map)
    return (entry_grad, (out_grad, in_grad, sum_grad, skip_part))


def block_finish(pack, partial_value, exit_grad, state_in, decay_rate):
    (
        input_map,
        output_map,
        step_size,
        decay_sum,
        within,
        mixing,
        inputs,
        to_end,
        weight_end,
        growth,
        local_state,
        carry,
        inner_out,
    ) = pack
    out_grad, in_grad, sum_grad, skip_part = partial_value
    exit_bf = exit_grad.astype(jnp.bfloat16)
    coef_grad = product("hnp,shp->hns", exit_bf, inputs)
    in_grad = in_grad + jnp.einsum("hns,hs->sn", coef_grad, weight_end, precision=highest)
    pulled = jnp.einsum("hns,sn->hs", coef_grad, input_map.astype(jnp.float32), precision=highest)
    end_weight = pulled * weight_end
    final_grad = jnp.sum(end_weight, axis=1) + carry * jnp.sum(exit_grad * state_in, axis=(1, 2))
    row_count = step_size.shape[1]
    last_mark = (jnp.arange(row_count) == row_count - 1).astype(jnp.float32)
    sum_grad = sum_grad - end_weight + final_grad[:, None] * last_mark[None, :]
    step_grad = jnp.cumsum(sum_grad[:, ::-1], axis=1)[:, ::-1]
    alog_part = decay_rate * jnp.sum(step_grad * step_size, axis=1)
    proj_grad = jnp.concatenate([in_grad, out_grad], axis=1).astype(jnp.bfloat16)
    return (proj_grad, alog_part, skip_part)


def chain_link(earlier, later):
    return (earlier[0] * later[0], later[1] + later[0][:, None, None] * earlier[1])


def local(hidden, values, targets, dt_raw, proj_weight, a_log, skip):
    row_count = hidden.shape[1]
    features = hidden[0]
    position = jnp.arange(row_count)
    lower_mask = (position[:, None] >= position[None, :]).astype(jnp.float32)
    picked = features
    projection = jnp.dot(
        picked,
        lax.all_gather(proj_weight, "fsdp", axis=0, tiled=True),
        preferred_element_type=jnp.float32,
    )
    proj_bf = projection.astype(jnp.bfloat16)
    step_size = jax.nn.softplus(dt_raw[0])
    decay_rate = -jnp.exp(a_log)
    sequences = lax.axis_size("fsdp")
    length = row_count * lax.axis_size("ctx")
    loss_scale = 1.0 / (values.shape[2] * math.sqrt(sequences * length))
    local_pack = block_local(proj_bf, step_size, decay_rate, values[0], lower_mask)
    carry = local_pack[11]
    local_state = local_pack[10]
    identity = (jnp.ones_like(carry), jnp.zeros_like(local_state))
    entry = prefix((carry, local_state), "ctx", chain_link, identity, False)
    state_in = entry[1]
    misfit, from_state, state_bf = block_output(local_pack, state_in, targets[0], skip)
    loss_part = 0.5 * loss_scale * jnp.sum(misfit * misfit)
    entry_grad, partial_value = block_return(local_pack, from_state, state_bf, misfit, loss_scale)
    later = prefix((carry, entry_grad), "ctx", chain_link, identity, True)
    proj_grad, alog_part, skip_part = block_finish(
        local_pack, partial_value, later[1], state_in, decay_rate
    )
    picked = features
    shard_grad = lax.psum_scatter(
        lax.dot_general(
            picked, proj_grad, (((0,), (0,)), ((), ())), preferred_element_type=jnp.float32
        ),
        "fsdp",
        scatter_dimension=0,
        tiled=True,
    )
    grad_w = lax.psum(shard_grad, "ctx")
    totals = lax.psum((loss_part, alog_part, skip_part), ("fsdp", "ctx"))
    return (grad_w, totals[1], totals[2], totals[0])


def solution(mesh):
    in_specs = (
        P("fsdp", "ctx", None),
        P("fsdp", "ctx", None),
        P("fsdp", "ctx", None),
        P("fsdp", None, "ctx"),
        P("fsdp", None),
        P(),
        P(),
    )
    out_specs = (P("fsdp", None), P(), P(), P())
    return jax.shard_map(local, mesh=mesh, in_specs=in_specs, out_specs=out_specs, check_vma=False)
```

profile of v0, /device:TPU:1, one launch (start us, length us, event | category | flops | bytes accessed | tf_op | source)
XLA Modules:
  0.0 1085.1 jit_solution(3268131084844295965)
XLA Ops:
  10.3 75.1 %all-gather.7.cloned.1.call-done = bf16[8192,128]{1,0:T(8,128)(2,1)} async-done(((bf16[512,128]{1,0:T(8,128)(2,1)}), bf16[8192,128]{1,0:T(8,128)(2,1)}) %all-gather.7.cloned.1.call-update) | async-done | bytes 2097168 | tf_op jit(solution)/shard_map/all_gather | solution.py:180
  92.0 84.0 %all-reduce = f32[1024]{0:T(1024)S(1)} all-reduce(f32[1024]{0:T(1024)S(1)} %dynamic-update-slice), channel_id=3, replica_groups=mesh['fsdp'=16,'ctx'=32] {'ctx'}, use_global_device_ids=true, to_apply=%add | all-reduce | flops 1024 | bytes 8192
  178.8 130.9 %all-gather.9.cloned.1.call-done = f32[1024,64,128]{2,1,0:T(8,128)} async-done(((f32[32,64,128]{2,1,0:T(8,128)}), f32[1024,64,128]{2,1,0:T(8,128)}) %all-gather.9.cloned.1.call-update) | async-done | bytes 33554448 | tf_op jit(solution)/shard_map/all_gather | solution.py:13
  309.7 46.7 %while.28 = (s32[]{:T(128)}, f32[32,64,128]{2,1,0:T(8,128)S(1)}, s32[]{:T(128)}, f32[32,32,64,128]{3,2,1,0:T(8,128)}, f32[32,32]{1,0:T(8,128)S(1)}, /*index=5*/s32[]{:T(128)}, s32[]{:T(128)}) while((s32[]{:T(128)}, f32[32,64,128]{2,1,0:T(8,128)S(1)}, s32[]{:T(128)}, f32[32,32,64,128]{3,2,1,0:T(8,128)}, f32[32,32]{1,0:T(8,128)S(1)}, ...), condition=%wide.region_2.3_spmd.clone, body=%wide.region_1.2_spmd.clone.sunk | while | flops 1048580 | bytes 3146225 | solution.py:25
  363.6 3.7 fusion.10
  367.8 204.4 %all-gather.11.cloned.1.call-done = f32[1024,64,128]{2,1,0:T(8,128)} async-done(((f32[32,64,128]{2,1,0:T(8,128)}), f32[1024,64,128]{2,1,0:T(8,128)}) %all-gather.11.cloned.1.call-update) | async-done | bytes 33554448 | tf_op jit(solution)/shard_map/all_gather | solution.py:13
  572.1 23.3 %rev.12 = f32[32,32,64,128]{3,2,1,0:T(8,128)} reverse(f32[32,32,64,128]{3,2,1,0:T(8,128)} %bitcast.108), dimensions={0} | reverse | bytes 67108864 | tf_op jit(solution)/shard_map/rev | solution.py:15
  595.4 85.1 %while.29 = (s32[]{:T(128)}, f32[32,64,128]{2,1,0:T(8,128)}, s32[]{:T(128)}, f32[32,32,64,128]{3,2,1,0:T(8,128)}, f32[32,32]{1,0:T(8,128)S(1)}, /*index=5*/s32[]{:T(128)}, s32[]{:T(128)}) while((s32[]{:T(128)}, f32[32,64,128]{2,1,0:T(8,128)}, s32[]{:T(128)}, f32[32,32,64,128]{3,2,1,0:T(8,128)}, f32[32,32]{1,0:T(8,128)S(1)}, ...), condition=%wide.region_5.6_spmd.clone, body=%wide.region_4.5_spmd.clone.sunk | while | flops 1048580 | bytes 3146225 | solution.py:25
  603.4 2.7 fusion.74
  608.9 2.7 fusion.74
  614.4 2.7 fusion.74
  619.9 2.7 fusion.74
  625.4 2.7 fusion.74
  630.9 2.7 fusion.74
  636.4 2.7 fusion.74
  655.7 2.7 fusion.74
  661.2 2.7 fusion.74
  666.8 2.7 fusion.74
  672.3 2.7 fusion.74
  677.8 2.7 fusion.74
  680.5 2.9 multiply_reduce_fusion.4
  690.8 97.0 %reduce-scatter.2.cloned.1.call-done = f32[512,128]{0,1:T(8,128)} async-done(((f32[8192,128]{0,1:T(8,128)}), f32[512,128]{0,1:T(8,128)}) %reduce-scatter.2.cloned.1.call-update) | async-done | bytes 262160 | tf_op jit(solution)/shard_map/reduce_scatter | solution.py:203
  788.0 98.9 %all-reduce.1 = (f32[32]{0:T(128)}, f32[32]{0:T(128)}, f32[]{:T(128)}) all-reduce(f32[32]{0:T(128)S(1)} %fusion.63, f32[32]{0:T(128)S(1)} %get-tuple-element.247, f32[]{:T(128)S(6)} %mul_shard_map.3), channel_id=1, replica_groups=mesh['fsdp'=16,'ctx'=32] {'fsdp','ctx'}, use_global_device_ids=true, to_apply=%region_15.16 | all-reduce | flops 65 | bytes 520 | tf_op jit(solution)/shard_map/psum | solution.py:212
  886.9 189.9 %all-reduce.4.cloned.1.call-done = f32[512,128]{0,1:T(8,128)} async-done(((f32[512,128]{0,1:T(8,128)}), f32[512,128]{0,1:T(8,128)}) %all-reduce.4.cloned.1.call-update) | async-done | bytes 262160 | tf_op jit(solution)/shard_map/psum | solution.py:211
  (181 shorter events, 125.8 us)
Async XLA Ops:
  7.2 78.2 %copy-start = (bf16[1,128,8192]{2,1,0:T(8,128)(2,1)S(1)}, bf16[1,128,8192]{2,1,0:T(8,128)(2,1)}, u32[]{:S(2)}) copy-start(bf16[1,128,8192]{2,1,0:T(8,128)(2,1)} %param.11) | copy-start | bytes 6291460
  7.2 2.4 copy-start.8
  7.2 2.5 copy-start.6
  7.2 78.2 %all-gather.7.cloned.1.call-start = ((), (), s32[]{:S(2)}) async-start(), calls=%async_computation.1 | async-start | bytes 2228224 | tf_op jit(solution)/shard_map/all_gather | solution.py:180
  7.9 301.7 %all-gather.9.cloned.1.call-start = ((), (), s32[]{:S(2)}) async-start(), calls=%async_computation.4 | async-start | bytes 34603008 | tf_op jit(solution)/shard_map/all_gather | solution.py:13
  9.6 78.3 %copy-start.1 = (bf16[1,128,4096]{1,2,0:T(8,128)(2,1)}, bf16[1,128,4096]{1,2,0:T(8,128)(2,1)S(1)}, u32[]{:S(2)}) copy-start(bf16[1,128,4096]{1,2,0:T(8,128)(2,1)S(1)} %copy.31) | copy-start | bytes 3145732
  89.7 482.4 %all-gather.11.cloned.1.call-start = ((), (), s32[]{:S(2)}) async-start(), calls=%async_computation.5 | async-start | bytes 34603008 | tf_op jit(solution)/shard_map/all_gather | solution.py:13
  356.4 1.2 copy-start.2
  356.4 1.9 copy-start.5
  356.4 1.9 copy-start.7
  360.7 1.4 copy-start.3
  363.5 424.3 %reduce-scatter.2.cloned.1.call-start = ((), (), s32[]{:S(2)}) async-start(), calls=%async_computation.2 | async-start | bytes 4456448 | tf_op jit(solution)/shard_map/reduce_scatter | solution.py:203
  363.6 3.8 copy-start.4
  686.2 390.5 %all-reduce.4.cloned.1.call-start = ((), (), s32[]{:S(2)}) async-start(), calls=%async_computation.3 | async-start | bytes 524288 | tf_op jit(solution)/shard_map/psum | solution.py:211
Sparse Core Ops, SparseCore 0:
  10.1 75.1 all-gather.6
  89.9 219.7 all-gather.8
  363.6 208.4 all-gather.10
  686.4 101.4 reduce-scatter.1
  790.6 286.1 all-reduce.3
where the time goes:
time: 1090 us
  waiting for transfers between devices  698 us (64%)
  blocking collectives  183 us (17%)
  other arithmetic  134 us (12%)
  local copies, waits for them, and re-layouts  34.6 us (3%)
  matrix products  18.7 us (2%)
  between operations  15.3 us (1%)
    all_gather x2, waiting for transfers between devices, prefix(): pieces = jax.tree.map(lambda part: lax.all_gather(part, axis), value)  335 us
    psum x1, waiting for transfers between devices, local(): grad_w = lax.psum(shard_grad, 'ctx')  190 us
    select_n x62, other arithmetic, hop(): jnp.where(position < mine, new, old)  130 us
    psum x1, blocking collectives, local(): totals = lax.psum((loss_part, alog_part, skip_part), ('fsdp', 'ctx'))  98.9 us
    reduce_scatter x1, waiting for transfers between devices, local(): lax.psum_scatter(lax.dot_general(picked, proj_grad, (((0,), (0,)), ((), (...  97 us
    unnamed x1, blocking collectives  84 us
    all_gather x1, waiting for transfers between devices, local(): lax.all_gather(proj_weight, 'fsdp', axis=0, tiled=True)  75.1 us
    rev x2, local copies, waits for them, and re-layouts, prefix(): pieces = jax.tree.map(lambda part: part[::-1], pieces)  23.3 us
  transfers between devices with their start and end apart: 5, of which 5 were waited for; matrix products, arithmetic and copies ran while one was open for 1% of the time, Pallas kernels for 0%

commit v1 on v0

v1 whole, which is shorter than its diff:
```python
import functools
import math

import jax
import jax.numpy as jnp
from jax import lax
from jax.experimental import pallas as pl
from jax.experimental.pallas import tpu as pltpu
from jax.sharding import PartitionSpec as P

HIGHEST = lax.Precision.HIGHEST
MESH = pl.DeviceIdType.MESH
F32 = jnp.float32
BF16 = jnp.bfloat16
T = 128
N = 64
ROW_CHIPS = 4


def dot(left, right):
    return jnp.dot(left, right, preferred_element_type=F32)


def dot_last(left, right):
    return lax.dot_general(left, right, (((1,), (1,)), ((), ())), preferred_element_type=F32)


def body(
    shards, blocks, scale,
    hid, val, tgt, dt, w, par, ow, osc,
    wbuf, hq, ws, dcb, bs, step_s, decay_s, fin_s, we_s, alog_s, skip_s, loss_s,
    carry_out, carry_in, l_out, l_in, s_out, s_in, e_out, e_in, x_out, x_in,
    sg, acc_c, acc_b, pg_out, pg_in, r_out, r_in, c_out, c_in, y_out, y_in, z_out, z_in,
    w_send, w_recv, v_send, v_recv, h_send, h_own, h_fwd, h_recv, k_send, k_recv,
    l_send, l_recv, s_send, s_recv, e_send, e_recv, x_send, x_recv,
    p_send, p_recv, r_send, r_recv, c_send, c_recv, y_send, y_recv, z_send, z_recv,
):
    heads = dt.shape[0]
    wide = w.shape[0]
    half = wide // 2
    chips = ROW_CHIPS
    octet = 2 * chips
    rows = blocks // octet
    f = lax.axis_index("fsdp")
    k = lax.axis_index("ctx")
    c = lax.rem(k, 2)
    o = lax.rem(k, octet)
    yh = lax.div(k, octet)
    x = lax.div(o, 2)
    first = yh * octet
    sib = k + 1 - 2 * c

    def ring(start, hop, count):
        return lax.rem(start + hop, count)

    def remote(src, dst, ss, rs, to_f, to_k):
        return pltpu.make_async_remote_copy(
            src_ref=src, dst_ref=dst, send_sem=ss, recv_sem=rs,
            device_id=(to_f, to_k), device_id_type=MESH,
        )

    def arrived(dst, rs):
        remote(dst, dst, rs, rs, f, sib).wait_recv()

    def left(src, ss):
        remote(src, src, ss, ss, f, sib).wait_send()

    def loop(count, fn, start=0):
        def step(i, carry):
            fn(i)
            return carry

        lax.fori_loop(start, count, step, 0)

    def lanes(i):
        return pl.ds(pl.multiple_of(i * T, T), T)

    barrier = pltpu.get_barrier_semaphore()

    def greet_f(j):
        pl.semaphore_signal(barrier, inc=1, device_id=(ring(f, j, shards), k), device_id_type=MESH)

    def greet_k(j):
        pl.semaphore_signal(barrier, inc=1, device_id=(f, ring(k, j, blocks)), device_id_type=MESH)

    loop(shards, greet_f, 1)
    loop(blocks, greet_k, 1)
    pl.semaphore_wait(barrier, shards + blocks - 2)

    def w_rows(g, core):
        return pl.ds(pl.multiple_of(g * wide + core * half, half), half)

    def w_go(j):
        remote(
            w.at[pl.ds(pl.multiple_of(c * half, half), half)], wbuf.at[w_rows(f, c)],
            w_send, w_recv.at[f], ring(f, j, shards), k,
        ).start()

    loop(shards, w_go, 1)

    step = jnp.maximum(dt[...], 0.0) + jnp.log1p(jnp.exp(-jnp.abs(dt[...])))
    row_id = lax.broadcasted_iota(jnp.int32, (T, T), 0)
    col_id = lax.broadcasted_iota(jnp.int32, (T, T), 1)
    upper = jnp.where(row_id <= col_id, 1.0, 0.0).astype(F32)
    decay = jnp.dot(-step * jnp.exp(par[0]), upper, precision=HIGHEST, preferred_element_type=F32)
    fin = jnp.broadcast_to(decay[:, T - 1 :], (heads, T))
    step_s[...] = step
    decay_s[...] = decay
    fin_s[...] = fin
    we_s[...] = jnp.exp(fin - decay) * step

    def carry_go(h):
        carry_out[h] = jnp.broadcast_to(jnp.exp(fin_s[pl.ds(h, 1), :]), (8, T))

        @pl.when(h != k)
        def _():
            remote(carry_out.at[h], carry_in.at[k], k_send, k_recv.at[k], f, h).start()

        @pl.when(h == k)
        def _():
            carry_in[h] = carry_out[h]

    loop(heads, carry_go)

    own_rows = pl.ds(pl.multiple_of(o * T, T), T)

    def h_go(i):
        for hop in range(1, chips):
            there = ring(x, hop, chips)
            remote(
                hid.at[:, pl.ds(pl.multiple_of(i * wide + there * T, T), T)], hq.at[own_rows, lanes(i)],
                h_send, h_recv.at[o], f, first + there * 2 + c,
            ).start()
        hq[own_rows, lanes(i)] = hid[:, pl.ds(pl.multiple_of(i * wide + x * T, T), T)]

    loop(shards, h_go)
    remote(hq.at[own_rows], hq.at[own_rows], h_own, h_recv.at[o], f, sib).start()

    lower = row_id >= col_id

    def head_start(h):
        drow = decay_s[pl.ds(h, 1), :]
        col = jnp.transpose(jnp.broadcast_to(drow, (T, T)))
        dcb[h] = col
        within = jnp.where(lower, jnp.exp(jnp.minimum(col - drow, 0.0)), 0.0)
        ws[h] = within * step_s[pl.ds(h, 1), :]
        gain = par[1, pl.ds(h, 1), :]
        bs[h] = gain * val[:, lanes(h)].astype(F32) - tgt[:, lanes(h)].astype(F32)

    loop(heads, head_start)

    def w_pass(j):
        g = ring(f, j, shards)
        slot = wbuf.at[w_rows(g, c)]
        arrived(slot, w_recv.at[g])
        remote(slot, slot, v_send, v_recv.at[g], f, sib).start()

    loop(shards, w_pass, 1)

    def hid_cols(g):
        return hid[:, pl.ds(pl.multiple_of(g * wide, wide), wide)]

    def w_use(j, total):
        g = ring(f, j, shards)
        arrived(wbuf.at[w_rows(g, 1 - c)], v_recv.at[g])
        return total + dot(hid_cols(g), wbuf[pl.ds(pl.multiple_of(g * wide, wide), wide), :])

    proj = lax.fori_loop(1, shards, w_use, dot(hid_cols(f), w[...]))
    proj = proj.astype(BF16).astype(F32)
    proj_t = jnp.transpose(proj)
    map_bt = proj_t[:N]
    map_b_t = proj_t[:N].astype(BF16)
    map_c_t = proj_t[N:].astype(BF16)
    map_c = proj[:, N:].astype(BF16)
    scores = dot(map_c, map_b_t)

    def head_local(h):
        v = val[:, lanes(h)]
        mixing = (ws[h] * scores).astype(BF16)
        coef = (map_bt * we_s[pl.ds(h, 1), :]).astype(BF16)
        both = dot(jnp.concatenate([mixing, coef], axis=0), v)
        bs[h] = bs[h] + both[:T]
        l_out[h] = both[T:].astype(BF16)

        @pl.when(h != k)
        def _():
            remote(l_out.at[h], l_in.at[k], l_send, l_recv.at[k], f, h).start()

        @pl.when(h == k)
        def _():
            l_in[h] = l_out[h]

    loop(heads, head_local)

    for hop in range(1, chips):
        j = ring(x, hop, chips) * 2 + c
        slab = hq.at[pl.ds(pl.multiple_of(j * T, T), T)]
        arrived(slab, h_recv.at[j])
        remote(slab, slab, h_fwd, h_recv.at[j], f, sib).start()

    def carry_wait(j):
        g = ring(k, j, blocks)
        arrived(carry_in.at[g], k_recv.at[g])

    loop(blocks, carry_wait, 1)

    def chain(came, out, back, in_sem, send_sem, back_sem, backward):
        def link(i, state):
            b = blocks - 1 - i if backward else i
            out[b] = state.astype(BF16)

            @pl.when(b != k)
            def _():
                remote(out.at[b], back.at[k], send_sem, back_sem.at[k], f, b).start()
                arrived(came.at[b], in_sem.at[b])

            @pl.when(b == k)
            def _():
                back[b] = out[b]

            return carry_in[b, 0:1, :] * state + came[b].astype(F32)

        lax.fori_loop(0, blocks, link, jnp.zeros((N, T), F32))

    chain(l_in, s_out, s_in, l_recv, s_send, s_recv, False)

    sg[...] = jnp.zeros_like(sg)
    acc_c[...] = jnp.zeros_like(acc_c)
    acc_b[...] = jnp.zeros_like(acc_b)

    def head_error(h):
        @pl.when(h != k)
        def _():
            arrived(s_in.at[h], s_recv.at[h])

        v = val[:, lanes(h)]
        state = s_in[h]
        col = dcb[h]
        growth = jnp.exp(col)
        grown_state = growth * dot(map_c, state)
        err = bs[h] + grown_state
        grad = err * scale
        loss_s[pl.ds(h, 1), :] = jnp.sum(err * err, axis=0, keepdims=True)
        skip_s[pl.ds(h, 1), :] = jnp.sum(grad * v.astype(F32), axis=0, keepdims=True)
        mix_grad = ws[h] * dot_last(grad.astype(BF16), v)
        sg[...] += mix_grad
        turn = mix_grad * scores * (col - decay_s[pl.ds(h, 1), :]) + grad * grown_state * col
        alog_s[pl.ds(h, 1), :] = jnp.sum(turn, axis=0, keepdims=True)
        grown = (growth * grad).astype(BF16)
        e_out[h] = dot(map_c_t, grown).astype(BF16)
        acc_c[...] += dot_last(state, grown)

        @pl.when(h != k)
        def _():
            remote(e_out.at[h], e_in.at[k], e_send, e_recv.at[k], f, h).start()

        @pl.when(h == k)
        def _():
            e_in[h] = e_out[h]

    loop(heads, head_error)
    chain(e_in, x_out, x_in, e_recv, x_send, x_recv, True)

    def head_exit(h):
        @pl.when(h != k)
        def _():
            arrived(x_in.at[h], x_recv.at[h])

        leaving = x_in[h]
        last = fin_s[pl.ds(h, 1), :]
        weighed = dot_last(leaving, val[:, lanes(h)]) * we_s[pl.ds(h, 1), :]
        acc_b[...] += weighed
        end = jnp.sum(weighed * map_bt, axis=0, keepdims=True)
        kept = jnp.sum(leaving.astype(F32) * s_in[h].astype(F32), axis=0, keepdims=True)
        alog_s[pl.ds(h, 1), :] += end * (last - decay_s[pl.ds(h, 1), :]) + last * jnp.exp(last) * kept

    loop(heads, head_exit)

    score_bf = sg[...].astype(BF16)
    pg_out[0] = (dot(map_c_t, score_bf) + acc_b[...]).astype(BF16)
    pg_out[1] = (dot_last(map_b_t, score_bf) + acc_c[...]).astype(BF16)
    own_cols = lanes(o)

    def pg_go(j):
        there = ring(o, j, octet)
        remote(
            pg_out.at[lax.rem(there, 2)], pg_in.at[:, own_cols], p_send, p_recv.at[o], f, first + there
        ).start()

    loop(octet, pg_go, 1)
    pg_in[:, own_cols] = pg_out[c]

    lane = lax.broadcasted_iota(jnp.int32, (heads, T), 1)
    alog = jnp.sum(alog_s[...], axis=1, keepdims=True)
    skip = jnp.sum(skip_s[...], axis=1, keepdims=True)
    loss = jnp.sum(loss_s[...], axis=1, keepdims=True) * (0.5 * scale)
    c_out[...] = jnp.where(lane == 0, alog, jnp.where(lane == 1, skip, jnp.where(lane == 2, loss, 0.0)))

    def c_go(j):
        remote(c_out, c_in.at[f], c_send, c_recv.at[f], ring(f, j, shards), k).start()

    loop(shards, c_go, 1)
    c_in[f] = c_out[...]

    def h_wait(j):
        src = j * 2 + 1 - c
        arrived(hq.at[pl.ds(pl.multiple_of(src * T, T), T)], h_recv.at[src])

    loop(chips, h_wait)

    def pg_wait(j):
        src = ring(o, j, octet)
        arrived(pg_in.at[:, lanes(src)], p_recv.at[src])

    loop(octet, pg_wait, 1)

    def r_go(j):
        g = ring(f, j, shards)
        r_out[g] = dot(pg_in[...], hq[:, lanes(g)]).astype(BF16)

        @pl.when(g != f)
        def _():
            remote(r_out.at[g], r_in.at[f], r_send, r_recv.at[f], g, k).start()

        @pl.when(g == f)
        def _():
            r_in[g] = r_out[g]

    loop(shards + 1, r_go, 1)

    def r_wait(j):
        g = ring(f, j, shards)
        arrived(r_in.at[g], r_recv.at[g])
        arrived(c_in.at[g], c_recv.at[g])

    loop(shards, r_wait, 1)
    y_out[0:N, :] = lax.fori_loop(0, shards, lambda i, s: s + r_in[i].astype(F32), jnp.zeros((N, T), F32))
    y_out[N:, :] = lax.fori_loop(0, shards, lambda i, s: s + c_in[i], jnp.zeros((heads, T), F32))

    for hop in range(1, rows):
        remote(y_out, y_in.at[yh], y_send.at[hop], y_recv.at[yh], f, ring(yh, hop, rows) * octet + o).start()
    y_in[yh] = y_out[...]
    for hop in range(1, rows):
        src = ring(yh, hop, rows)
        arrived(y_in.at[src], y_recv.at[src])
    total = y_in[0]
    for i in range(1, rows):
        total = total + y_in[i]
    z_out[...] = total

    def z_go(j):
        remote(z_out, z_in.at[o], z_send, z_recv.at[o], f, first + ring(o, j, octet)).start()

    loop(octet, z_go, 1)
    z_in[o] = z_out[...]

    def z_wait(j):
        src = ring(o, j, octet)
        arrived(z_in.at[src], z_recv.at[src])

    loop(octet, z_wait, 1)
    for i in range(chips):
        ow[i * T : (i + 1) * T, :] = jnp.transpose(
            jnp.concatenate([z_in[2 * i, 0:N, :], z_in[2 * i + 1, 0:N, :]], axis=0)
        )
    sums = z_in[0, N:, :]
    for i in range(1, octet):
        sums = sums + z_in[i, N:, :]
    osc[...] = sums

    others = pl.ds(0, blocks - 1)
    peers = pl.ds(0, shards - 1)
    left(wbuf.at[pl.ds(0, (shards - 1) * half)], w_send)
    left(wbuf.at[pl.ds(0, (shards - 1) * half)], v_send)
    left(hq.at[pl.ds(0, (chips - 1) * T)], h_send)
    left(hq.at[pl.ds(0, T)], h_own)
    left(hq.at[pl.ds(0, (chips - 1) * T)], h_fwd)
    left(carry_out.at[others], k_send)
    left(l_out.at[others], l_send)
    left(s_out.at[others], s_send)
    left(e_out.at[others], e_send)
    left(x_out.at[others], x_send)
    left(pg_in.at[:, pl.ds(0, (octet - 1) * T)], p_send)
    left(r_out.at[peers], r_send)
    left(c_in.at[peers], c_send)
    for hop in range(1, rows):
        left(y_out, y_send.at[hop])
    left(z_in.at[pl.ds(0, octet - 1)], z_send)


def local(hidden, values, targets, dt_raw, proj_weight, a_log, skip):
    shards = lax.axis_size("fsdp")
    blocks = lax.axis_size("ctx")
    heads = a_log.shape[0]
    wide, both = proj_weight.shape
    octet = 2 * ROW_CHIPS
    rows = blocks // octet
    scale = 1.0 / (values.shape[2] * math.sqrt(shards * hidden.shape[1] * blocks))
    par = jnp.broadcast_to(jnp.stack([a_log, skip])[:, :, None], (2, heads, T))
    vmem = pltpu.VMEM
    per_head = lambda kind: vmem((heads, N, T), kind)
    small = vmem((heads, T), F32)
    one = pltpu.SemaphoreType.DMA
    many = lambda n: pltpu.SemaphoreType.DMA((n,))
    scratch = [
        vmem((shards * wide, both), BF16),
        vmem((octet * T, shards * T), BF16),
        vmem((heads, T, T), F32), vmem((heads, T, T), F32), vmem((heads, T, T), F32),
        small, small, small, small, small, small, small,
        vmem((heads, 8, T), F32), vmem((blocks, 8, T), F32),
        *[per_head(BF16)] * 8,
        vmem((T, T), F32), vmem((N, T), F32), vmem((N, T), F32),
        vmem((2, N, T), BF16), vmem((N, octet * T), BF16),
        vmem((shards, N, T), BF16), vmem((shards, N, T), BF16),
        small, vmem((shards, heads, T), F32),
        vmem((N + heads, T), F32), vmem((rows, N + heads, T), F32),
        vmem((N + heads, T), F32), vmem((octet, N + heads, T), F32),
        one, many(shards), one, many(shards), one, one, one, many(octet), one, many(blocks),
        *[one, many(blocks)] * 4,
        one, many(octet), one, many(shards), one, many(shards), many(rows), many(rows), one, many(octet),
    ]
    spec = pl.BlockSpec(memory_space=vmem)
    grad_w, sums = pl.pallas_call(
        functools.partial(body, shards, blocks, scale),
        out_shape=(
            jax.ShapeDtypeStruct((wide, both), F32),
            jax.ShapeDtypeStruct((heads, T), F32),
        ),
        in_specs=[spec] * 6,
        out_specs=(spec, spec),
        scratch_shapes=scratch,
        compiler_params=pltpu.CompilerParams(
            collective_id=0, has_side_effects=True, vmem_limit_bytes=48 * 2**20
        ),
    )(hidden[0], values[0], targets[0], dt_raw[0], proj_weight, par)
    return (grad_w, sums[:, 0], sums[:, 1], jnp.sum(sums[:, 2]))


def solution(mesh):
    in_specs = (
        P("fsdp", "ctx", None),
        P("fsdp", "ctx", None),
        P("fsdp", "ctx", None),
        P("fsdp", None, "ctx"),
        P("fsdp", None),
        P(),
        P(),
    )
    out_specs = (P("fsdp", None), P(), P(), P())
    return jax.shard_map(local, mesh=mesh, in_specs=in_specs, out_specs=out_specs, check_vma=False)
```

time: 1090 us -> 147 us (0.13)
  waiting for transfers between devices: 698 us -> 0 us
  blocking collectives: 183 us -> 0 us
  Pallas kernels: 0 us -> 137 us
  other arithmetic: 134 us -> 1.41 us
  local copies, waits for them, and re-layouts: 34.6 us -> 6.44 us
  matrix products: 18.7 us -> 0 us
  between operations: 15.3 us -> 0.65 us
    all_gather x3 -> x0, waiting for transfers between devices: 410 us -> none  [the longest x2 335 us: prefix(): pieces = jax.tree.map(lambda part: lax.all_gather(part, axis), value)]
    psum x1 -> x0, waiting for transfers between devices: 190 us -> none  [local(): grad_w = lax.psum(shard_grad, 'ctx')]
    pallas_call x0 -> x1, Pallas kernels: none -> 137 us  [local(): pl.pallas_call(functools.partial(body, shards, blocks, scale), out_shape=...]
    select_n x63 -> x0, other arithmetic: 130 us -> none  [the longest x62 130 us: hop(): jnp.where(position < mine, new, old)]
    psum x1 -> x0, blocking collectives: 98.9 us -> none  [local(): totals = lax.psum((loss_part, alog_part, skip_part), ('fsdp', 'ctx'))]
    reduce_scatter x1 -> x0, waiting for transfers between devices: 97 us -> none  [local(): lax.psum_scatter(lax.dot_general(picked, proj_grad, (((0,), (0,)), ((), (...]
    unnamed x1 -> x0, blocking collectives: 84 us -> none
    rev x4 -> x0, local copies, waits for them, and re-layouts: 23.4 us -> none  [the longest x2 23.3 us: prefix(): pieces = jax.tree.map(lambda part: part[::-1], pieces)]
  transfers between devices with their start and end apart: 5 -> 0, of which waited for: 5 -> 0; matrix products, arithmetic and copies ran while one was open for 1% -> 0% of each run, Pallas kernels for 0% -> 0%
where the time goes in v1:
time: 147 us; the launch traced here: 146 us
  Pallas kernels  137 us (93%)
  local copies, waits for them, and re-layouts  6.44 us (4%)
    pallas_call x1, Pallas kernels, local(): pl.pallas_call(functools.partial(body, shards, blocks, scale), out_shape=...  137 us
    unnamed x11, local copies, waits for them, and re-layouts  6.37 us

profile of v1, /device:TPU:1, one launch (start us, length us, event | category | flops | bytes accessed | tf_op | source)
XLA Modules:
  0.0 145.8 jit_solution(2788651767405532890)
XLA Ops:
  0.6 0.7 pad_maximum_fusion
  1.3 0.1 broadcast_in_dim.2.par
  1.4 0.0 copy-start
  1.4 1.6 %copy-done = bf16[1,128,8192]{2,1,0:T(8,128)(2,1)S(1)} copy-done((bf16[1,128,8192]{2,1,0:T(8,128)(2,1)S(1)}, bf16[1,128,8192]{2,1,0:T(8,128)(2,1)}, u32[]{:S(2)}) %copy-start) | copy-done | bytes 2097176
  3.0 0.0 copy-start.1
  3.0 1.2 copy-done.1
  4.2 0.0 copy-start.2
  4.2 1.2 copy-done.2
  5.4 0.0 copy-start.3
  5.4 0.9 copy-done.3
  6.3 0.0 copy-start.4
  6.3 0.7 copy-done.4
  7.1 137.3 %shard_map.102 = (f32[512,128]{1,0:T(8,128)S(1)}, f32[32,128]{1,0:T(8,128)S(1)}) custom-call(bf16[128,8192]{1,0:T(8,128)(2,1)S(1)} %bitcast.6, bf16[128,4096]{1,0:T(8,128)(2,1)S(1)} %bitcast.7, bf16[128,4096]{1,0:T(8,128)(2,1)S(1)} %bitcast.8, f32[32,128]{1,0:T(8,128)S(1)} %bitcast.9, bf16[512,128]{1,0:T(8,128)(2,1)S(1)} %copy-done.3, ...), custom_call_target="tpu_custom_call" | custom-call | tf_op jit(solution)/shard_map/pallas_call | solution.py:423
  144.3 0.7 slice_reduce_fusion
  145.0 0.7 copy.12
Async XLA Ops:
  1.4 1.6 %copy-start = (bf16[1,128,8192]{2,1,0:T(8,128)(2,1)S(1)}, bf16[1,128,8192]{2,1,0:T(8,128)(2,1)}, u32[]{:S(2)}) copy-start(bf16[1,128,8192]{2,1,0:T(8,128)(2,1)} %param.7) | copy-start | bytes 6291460
  3.0 1.2 copy-start.1
  4.2 1.2 copy-start.2
  5.4 0.9 copy-start.3
  6.3 0.7 copy-start.4

commit v2 on v1

--- a/solution.py
+++ b/solution.py
@@ -27,17 +27,17 @@
 
 def body(
     shards, blocks, scale,
-    hid, val, tgt, dt, w, par, ow, osc,
-    wbuf, hq, ws, dcb, bs, step_s, decay_s, fin_s, we_s, alog_s, skip_s, loss_s,
+    hid_h, val_h, tgt_h, dt_h, w_h, a_ref, skip_ref, ow, osc,
+    hid, val, tgt, dt, w, in_sem, wbuf, hq, ws, dcb, bs, rate_s, step_s, decay_s, fin_s, we_s, alog_s, skip_s, loss_s,
     carry_out, carry_in, l_out, l_in, s_out, s_in, e_out, e_in, x_out, x_in,
     sg, acc_c, acc_b, pg_out, pg_in, r_out, r_in, c_out, c_in, y_out, y_in, z_out, z_in,
-    w_send, w_recv, v_send, v_recv, h_send, h_own, h_fwd, h_recv, k_send, k_recv,
+    w_send, w_recv, v_send, v_recv, u_send, h_send, h_far, h_own, h_fwd, h_recv, k_send, k_recv,
     l_send, l_recv, s_send, s_recv, e_send, e_recv, x_send, x_recv,
     p_send, p_recv, r_send, r_recv, c_send, c_recv, y_send, y_recv, z_send, z_recv,
 ):
     heads = dt.shape[0]
     wide = w.shape[0]
-    half = wide // 2
+    part = wide // (2 * ROW_CHIPS)
     chips = ROW_CHIPS
     octet = 2 * chips
     rows = blocks // octet
@@ -85,24 +85,34 @@
 
     loop(shards, greet_f, 1)
     loop(blocks, greet_k, 1)
+    loads = [
+        pltpu.make_async_copy(src, dst, in_sem.at[i])
+        for i, (src, dst) in enumerate(((w_h, w), (dt_h, dt), (val_h, val), (tgt_h, tgt), (hid_h, hid)))
+    ]
+    for load in loads:
+        load.start()
+    loads[0].wait()
     pl.semaphore_wait(barrier, shards + blocks - 2)
 
-    def w_rows(g, core):
-        return pl.ds(pl.multiple_of(g * wide + core * half, half), half)
+    own_part = pl.ds(pl.multiple_of(o * part, part), part)
 
     def w_go(j):
-        remote(
-            w.at[pl.ds(pl.multiple_of(c * half, half), half)], wbuf.at[w_rows(f, c)],
-            w_send, w_recv.at[f], ring(f, j, shards), k,
-        ).start()
+        remote(w.at[own_part], wbuf.at[f, own_part], w_send, w_recv.at[f], ring(f, j, shards), k).start()
 
     loop(shards, w_go, 1)
-
+    wbuf[f, own_part, :] = w[own_part, :]
+
+    loads[1].wait()
+
+    def spread(h):
+        rate_s[pl.ds(h, 1), :] = jnp.full((1, T), a_ref[h], F32)
+
+    loop(heads, spread)
     step = jnp.maximum(dt[...], 0.0) + jnp.log1p(jnp.exp(-jnp.abs(dt[...])))
     row_id = lax.broadcasted_iota(jnp.int32, (T, T), 0)
     col_id = lax.broadcasted_iota(jnp.int32, (T, T), 1)
     upper = jnp.where(row_id <= col_id, 1.0, 0.0).astype(F32)
-    decay = jnp.dot(-step * jnp.exp(par[0]), upper, precision=HIGHEST, preferred_element_type=F32)
+    decay = jnp.dot(-step * jnp.exp(rate_s[...]), upper, precision=HIGHEST, preferred_element_type=F32)
     fin = jnp.broadcast_to(decay[:, T - 1 :], (heads, T))
     step_s[...] = step
     decay_s[...] = decay
@@ -122,20 +132,48 @@
 
     loop(heads, carry_go)
 
+    def w_pass(j):
+        g = ring(f, shards - j, shards)
+        slot = wbuf.at[g, own_part]
+
+        @pl.when(j > 0)
+        def _():
+            arrived(slot, w_recv.at[g])
+
+        for hop in range(1, chips):
+            there = first + ring(x, hop, chips) * 2 + c
+            remote(slot, slot, v_send, v_recv.at[o], f, there).start()
+
+    loop(shards, w_pass)
+    own_slab = wbuf.at[:, own_part]
+    remote(own_slab, own_slab, u_send, v_recv.at[o], f, sib).start()
+
     own_rows = pl.ds(pl.multiple_of(o * T, T), T)
 
-    def h_go(i):
-        for hop in range(1, chips):
-            there = ring(x, hop, chips)
-            remote(
-                hid.at[:, pl.ds(pl.multiple_of(i * wide + there * T, T), T)], hq.at[own_rows, lanes(i)],
-                h_send, h_recv.at[o], f, first + there * 2 + c,
-            ).start()
+    def hid_to(i, hop, sem):
+        there = ring(x, hop, chips)
+        remote(
+            hid.at[:, pl.ds(pl.multiple_of(i * wide + there * T, T), T)], hq.at[own_rows, lanes(i)],
+            sem, h_recv.at[o], f, first + there * 2 + c,
+        ).start()
+
+    loads[4].wait()
+
+    def h_near(i):
+        hid_to(i, 1, h_send)
+        if chips > 2:
+            hid_to(i, chips - 1, h_send)
         hq[own_rows, lanes(i)] = hid[:, pl.ds(pl.multiple_of(i * wide + x * T, T), T)]
 
-    loop(shards, h_go)
+    def h_away(i):
+        for hop in range(2, chips - 1):
+            hid_to(i, hop, h_far)
+
+    loop(shards, h_near)
     remote(hq.at[own_rows], hq.at[own_rows], h_own, h_recv.at[o], f, sib).start()
 
+    loads[2].wait()
+    loads[3].wait()
     lower = row_id >= col_id
 
     def head_start(h):
@@ -144,28 +182,24 @@
         dcb[h] = col
         within = jnp.where(lower, jnp.exp(jnp.minimum(col - drow, 0.0)), 0.0)
         ws[h] = within * step_s[pl.ds(h, 1), :]
-        gain = par[1, pl.ds(h, 1), :]
-        bs[h] = gain * val[:, lanes(h)].astype(F32) - tgt[:, lanes(h)].astype(F32)
+        bs[h] = skip_ref[h] * val[:, lanes(h)].astype(F32) - tgt[:, lanes(h)].astype(F32)
 
     loop(heads, head_start)
 
-    def w_pass(j):
-        g = ring(f, j, shards)
-        slot = wbuf.at[w_rows(g, c)]
-        arrived(slot, w_recv.at[g])
-        remote(slot, slot, v_send, v_recv.at[g], f, sib).start()
-
-    loop(shards, w_pass, 1)
-
-    def hid_cols(g):
-        return hid[:, pl.ds(pl.multiple_of(g * wide, wide), wide)]
-
-    def w_use(j, total):
-        g = ring(f, j, shards)
-        arrived(wbuf.at[w_rows(g, 1 - c)], v_recv.at[g])
-        return total + dot(hid_cols(g), wbuf[pl.ds(pl.multiple_of(g * wide, wide), wide), :])
-
-    proj = lax.fori_loop(1, shards, w_use, dot(hid_cols(f), w[...]))
+    def slab(src):
+        return wbuf.at[:, pl.ds(pl.multiple_of(src * part, part), part)]
+
+    for hop in range(1, chips):
+        src = ring(x, hop, chips) * 2 + c
+        arrived(slab(src), v_recv.at[src])
+        remote(slab(src), slab(src), u_send, v_recv.at[src], f, sib).start()
+
+    def w_rest(j):
+        src = j * 2 + 1 - c
+        arrived(slab(src), v_recv.at[src])
+
+    loop(chips, w_rest)
+    proj = dot(hid[...], wbuf[...].reshape(shards * wide, 2 * N))
     proj = proj.astype(BF16).astype(F32)
     proj_t = jnp.transpose(proj)
     map_bt = proj_t[:N]
@@ -174,7 +208,8 @@
     map_c = proj[:, N:].astype(BF16)
     scores = dot(map_c, map_b_t)
 
-    def head_local(h):
+    def head_local(j):
+        h = ring(k, j, heads)
         v = val[:, lanes(h)]
         mixing = (ws[h] * scores).astype(BF16)
         coef = (map_bt * we_s[pl.ds(h, 1), :]).astype(BF16)
@@ -190,13 +225,8 @@
         def _():
             l_in[h] = l_out[h]
 
-    loop(heads, head_local)
-
-    for hop in range(1, chips):
-        j = ring(x, hop, chips) * 2 + c
-        slab = hq.at[pl.ds(pl.multiple_of(j * T, T), T)]
-        arrived(slab, h_recv.at[j])
-        remote(slab, slab, h_fwd, h_recv.at[j], f, sib).start()
+    loop(heads + 1, head_local, 1)
+    loop(shards, h_away)
 
     def carry_wait(j):
         g = ring(k, j, blocks)
@@ -211,16 +241,18 @@
 
             @pl.when(b != k)
             def _():
-                remote(out.at[b], back.at[k], send_sem, back_sem.at[k], f, b).start()
                 arrived(came.at[b], in_sem.at[b])
 
-            @pl.when(b == k)
-            def _():
-                back[b] = out[b]
-
             return carry_in[b, 0:1, :] * state + came[b].astype(F32)
 
         lax.fori_loop(0, blocks, link, jnp.zeros((N, T), F32))
+
+        def give(j):
+            b = ring(k, j, blocks)
+            remote(out.at[b], back.at[k], send_sem, back_sem.at[k], f, b).start()
+
+        loop(blocks, give, 1)
+        back[k] = out[k]
 
     chain(l_in, s_out, s_in, l_recv, s_send, s_recv, False)
 
@@ -228,7 +260,9 @@
     acc_c[...] = jnp.zeros_like(acc_c)
     acc_b[...] = jnp.zeros_like(acc_b)
 
-    def head_error(h):
+    def head_error(j):
+        h = ring(k, heads - j, heads)
+
         @pl.when(h != k)
         def _():
             arrived(s_in.at[h], s_recv.at[h])
@@ -258,10 +292,19 @@
         def _():
             e_in[h] = e_out[h]
 
-    loop(heads, head_error)
+    loop(heads + 1, head_error, 1)
+
+    for hop in range(1, chips):
+        j = ring(x, hop, chips) * 2 + c
+        piece = hq.at[pl.ds(pl.multiple_of(j * T, T), T)]
+        arrived(piece, h_recv.at[j])
+        remote(piece, piece, h_fwd, h_recv.at[j], f, sib).start()
+
     chain(e_in, x_out, x_in, e_recv, x_send, x_recv, True)
 
-    def head_exit(h):
+    def head_exit(j):
+        h = ring(k, heads - j, heads)
+
         @pl.when(h != k)
         def _():
             arrived(x_in.at[h], x_recv.at[h])
@@ -274,7 +317,7 @@
         kept = jnp.sum(leaving.astype(F32) * s_in[h].astype(F32), axis=0, keepdims=True)
         alog_s[pl.ds(h, 1), :] += end * (last - decay_s[pl.ds(h, 1), :]) + last * jnp.exp(last) * kept
 
-    loop(heads, head_exit)
+    loop(heads + 1, head_exit, 1)
 
     score_bf = sg[...].astype(BF16)
     pg_out[0] = (dot(map_c_t, score_bf) + acc_b[...]).astype(BF16)
@@ -370,9 +413,12 @@
 
     others = pl.ds(0, blocks - 1)
     peers = pl.ds(0, shards - 1)
-    left(wbuf.at[pl.ds(0, (shards - 1) * half)], w_send)
-    left(wbuf.at[pl.ds(0, (shards - 1) * half)], v_send)
-    left(hq.at[pl.ds(0, (chips - 1) * T)], h_send)
+    left(wbuf.at[peers, pl.ds(0, part)], w_send)
+    left(wbuf.at[:, pl.ds(0, (chips - 1) * part)], v_send)
+    left(wbuf.at[:, pl.ds(0, chips * part)], u_send)
+    left(hq.at[pl.ds(0, min(2, chips - 1) * T)], h_send)
+    if chips > 3:
+        left(hq.at[pl.ds(0, (chips - 3) * T)], h_far)
     left(hq.at[pl.ds(0, T)], h_own)
     left(hq.at[pl.ds(0, (chips - 1) * T)], h_fwd)
     left(carry_out.at[others], k_send)
@@ -396,17 +442,18 @@
     octet = 2 * ROW_CHIPS
     rows = blocks // octet
     scale = 1.0 / (values.shape[2] * math.sqrt(shards * hidden.shape[1] * blocks))
-    par = jnp.broadcast_to(jnp.stack([a_log, skip])[:, :, None], (2, heads, T))
     vmem = pltpu.VMEM
     per_head = lambda kind: vmem((heads, N, T), kind)
     small = vmem((heads, T), F32)
     one = pltpu.SemaphoreType.DMA
     many = lambda n: pltpu.SemaphoreType.DMA((n,))
     scratch = [
-        vmem((shards * wide, both), BF16),
+        vmem(hidden.shape[1:], BF16), vmem(values.shape[1:], BF16), vmem(targets.shape[1:], BF16),
+        small, vmem((wide, both), BF16), many(5),
+        vmem((shards, wide, both), BF16),
         vmem((octet * T, shards * T), BF16),
         vmem((heads, T, T), F32), vmem((heads, T, T), F32), vmem((heads, T, T), F32),
-        small, small, small, small, small, small, small,
+        *[small] * 8,
         vmem((heads, 8, T), F32), vmem((blocks, 8, T), F32),
         *[per_head(BF16)] * 8,
         vmem((T, T), F32), vmem((N, T), F32), vmem((N, T), F32),
@@ -415,7 +462,7 @@
         small, vmem((shards, heads, T), F32),
         vmem((N + heads, T), F32), vmem((rows, N + heads, T), F32),
         vmem((N + heads, T), F32), vmem((octet, N + heads, T), F32),
-        one, many(shards), one, many(shards), one, one, one, many(octet), one, many(blocks),
+        one, many(shards), one, many(octet), one, one, one, one, one, many(octet), one, many(blocks),
         *[one, many(blocks)] * 4,
         one, many(octet), one, many(shards), one, many(shards), many(rows), many(rows), one, many(octet),
     ]
@@ -426,13 +473,13 @@
             jax.ShapeDtypeStruct((wide, both), F32),
             jax.ShapeDtypeStruct((heads, T), F32),
         ),
-        in_specs=[spec] * 6,
+        in_specs=[pl.BlockSpec(memory_space=pltpu.HBM)] * 5 + [pl.BlockSpec(memory_space=pltpu.SMEM)] * 2,
         out_specs=(spec, spec),
         scratch_shapes=scratch,
         compiler_params=pltpu.CompilerParams(
-            collective_id=0, has_side_effects=True, vmem_limit_bytes=48 * 2**20
+            collective_id=0, has_side_effects=True, vmem_limit_bytes=56 * 2**20
         ),
-    )(hidden[0], values[0], targets[0], dt_raw[0], proj_weight, par)
+    )(hidden[0], values[0], targets[0], dt_raw[0], proj_weight, a_log, skip)
     return (grad_w, sums[:, 0], sums[:, 1], jnp.sum(sums[:, 2]))
 
 

time: 147 us -> 143 us (0.973)
  local copies, waits for them, and re-layouts: 6.44 us -> 1.67 us
  Pallas kernels: 137 us -> 139 us
    unnamed x11 -> x1, local copies, waits for them, and re-layouts: 6.37 us -> 1.67 us
    pallas_call x1, Pallas kernels: 137 us -> 139 us  [local(): pl.pallas_call(functools.partial(body, shards, blocks, scale), out_shape=...]
where the time goes in v2:
time: 143 us
  Pallas kernels  139 us (97%)
  local copies, waits for them, and re-layouts  1.67 us (1%)
  other arithmetic  1.56 us (1%)
    pallas_call x1, Pallas kernels, local(): pl.pallas_call(functools.partial(body, shards, blocks, scale), out_shape=...  139 us

profile of v2, /device:TPU:1, one launch (start us, length us, event | category | flops | bytes accessed | tf_op | source)
XLA Modules:
  0.0 142.8 jit_solution(17862780322426500977)
XLA Ops:
  0.6 138.9 %shard_map.102 = (f32[512,128]{1,0:T(8,128)}, f32[32,128]{1,0:T(8,128)}) custom-call(bf16[128,8192]{1,0:T(8,128)(2,1)} %bitcast.4, bf16[128,4096]{1,0:T(8,128)(2,1)} %bitcast.5, bf16[128,4096]{1,0:T(8,128)(2,1)} %bitcast.6, f32[32,128]{1,0:T(8,128)} %bitcast.7, bf16[512,128]{1,0:T(8,128)(2,1)} %w_h.1, f32[32]{0:T(128)} %a_ref.1, f32[32]{0:T(128)} %skip_ref.1), custom_call_target="tpu_custom_call" | custom-call | tf_op jit(solution)/shard_map/pallas_call | solution.py:470
  139.6 1.6 %slice_reduce_fusion = (f32[]{:T(128)}, f32[32]{0:T(128)}, f32[32]{0:T(128)}) fusion(f32[32,128]{1,0:T(8,128)} %get-tuple-element.7), kind=kLoop, calls=%fused_computation | loop fusion | flops 31 | bytes 644 | tf_op jit(solution)/shard_map/reduce_sum | solution.py:483
  141.2 1.7 %copy.12 = f32[512,128]{1,0:T(8,128)} copy(f32[512,128]{1,0:T(8,128)} %get-tuple-element.15) | data formatting | bytes 524288

commit v3 on v2

--- a/solution.py
+++ b/solution.py
@@ -14,6 +14,7 @@
 BF16 = jnp.bfloat16
 T = 128
 N = 64
+GROUP = 4
 ROW_CHIPS = 4
 
 
@@ -29,11 +30,15 @@
     shards, blocks, scale,
     hid_h, val_h, tgt_h, dt_h, w_h, a_ref, skip_ref, ow, osc,
     hid, val, tgt, dt, w, in_sem, wbuf, hq, ws, dcb, bs, rate_s, step_s, decay_s, fin_s, we_s, alog_s, skip_s, loss_s,
-    carry_out, carry_in, l_out, l_in, s_out, s_in, e_out, e_in, x_out, x_in,
-    sg, acc_c, acc_b, pg_out, pg_in, r_out, r_in, c_out, c_in, y_out, y_in, z_out, z_in,
-    w_send, w_recv, v_send, v_recv, u_send, h_send, h_far, h_own, h_fwd, h_recv, k_send, k_recv,
+    fin_sib, early_s, late_s, carry_out, carry_in,
+    l_out, l_sib, s_raw, s_pass, s_in, e_out, e_sib, x_raw, x_pass, x_in,
+    l_pair, l_in, s_out, e_pair, e_in, x_out,
+    sg, acc_c, acc_b, pg_out, pg_in, r_out, r_in, c_out, c_in, y_out, y_in, z_out, z_in, d_out, d_in, t_out, t_in,
+    w_send, w_recv, v_send, v_recv, u_send, h_send, h_far, h_own, h_fwd, h_recv, n_send, n_recv, k_send, k_recv,
     l_send, l_recv, s_send, s_recv, e_send, e_recv, x_send, x_recv,
+    lp_send, lp_recv, sp_send, sp_recv, ep_send, ep_recv, xp_send, xp_recv,
     p_send, p_recv, r_send, r_recv, c_send, c_recv, y_send, y_recv, z_send, z_recv,
+    d_send, d_recv, t_send, t_recv,
 ):
     heads = dt.shape[0]
     wide = w.shape[0]
@@ -49,6 +54,18 @@
     x = lax.div(o, 2)
     first = yh * octet
     sib = k + 1 - 2 * c
+    pairs = blocks // 2
+    q = lax.div(k, 2)
+
+    def mine(p):
+        return 2 * p + c
+
+    def theirs(p):
+        return 2 * p + 1 - c
+
+    def by_core(own_first, own_second):
+        return jnp.where(c == 0, own_first, own_second)
+
 
     def ring(start, hop, count):
         return lax.rem(start + hop, count)
@@ -119,18 +136,7 @@
     fin_s[...] = fin
     we_s[...] = jnp.exp(fin - decay) * step
 
-    def carry_go(h):
-        carry_out[h] = jnp.broadcast_to(jnp.exp(fin_s[pl.ds(h, 1), :]), (8, T))
-
-        @pl.when(h != k)
-        def _():
-            remote(carry_out.at[h], carry_in.at[k], k_send, k_recv.at[k], f, h).start()
-
-        @pl.when(h == k)
-        def _():
-            carry_in[h] = carry_out[h]
-
-    loop(heads, carry_go)
+    remote(fin_s, fin_sib, n_send, n_recv, f, sib).start()
 
     def w_pass(j):
         g = ring(f, shards - j, shards)
@@ -147,6 +153,25 @@
     loop(shards, w_pass)
     own_slab = wbuf.at[:, own_part]
     remote(own_slab, own_slab, u_send, v_recv.at[o], f, sib).start()
+
+    arrived(fin_sib, n_recv)
+    early_s[...] = jnp.exp(by_core(fin_s[...], fin_sib[...]))
+    late_s[...] = jnp.exp(by_core(fin_sib[...], fin_s[...]))
+
+    def carry_go(p):
+        h = mine(p)
+        both = early_s[pl.ds(h, 1), :] * late_s[pl.ds(h, 1), :]
+        carry_out[p] = jnp.broadcast_to(both, (8, T))
+
+        @pl.when(p != q)
+        def _():
+            remote(carry_out.at[p], carry_in.at[q], k_send, k_recv.at[q], f, h).start()
+
+        @pl.when(p == q)
+        def _():
+            carry_in[p] = carry_out[p]
+
+    loop(pairs, carry_go)
 
     own_rows = pl.ds(pl.multiple_of(o * T, T), T)
 
@@ -176,7 +201,11 @@
     loads[3].wait()
     lower = row_id >= col_id
 
-    def head_start(h):
+    def head_start(i):
+        for u in range(GROUP):
+            head_start_one(i * GROUP + u)
+
+    def head_start_one(h):
         drow = decay_s[pl.ds(h, 1), :]
         col = jnp.transpose(jnp.broadcast_to(drow, (T, T)))
         dcb[h] = col
@@ -184,7 +213,7 @@
         ws[h] = within * step_s[pl.ds(h, 1), :]
         bs[h] = skip_ref[h] * val[:, lanes(h)].astype(F32) - tgt[:, lanes(h)].astype(F32)
 
-    loop(heads, head_start)
+    loop(heads // GROUP, head_start)
 
     def slab(src):
         return wbuf.at[:, pl.ds(pl.multiple_of(src * part, part), part)]
@@ -208,8 +237,41 @@
     map_c = proj[:, N:].astype(BF16)
     scores = dot(map_c, map_b_t)
 
-    def head_local(j):
-        h = ring(k, j, heads)
+    def target(group, u):
+        return ring(q, group * GROUP + u + 1, pairs)
+
+    def origin(group, u):
+        return ring(q, pairs - 1 - group * GROUP - u, pairs)
+
+    def hand_over(p, out, come, send_sem, recv_sem):
+        @pl.when(p != q)
+        def _():
+            remote(out.at[p], come.at[q], send_sem, recv_sem.at[q], f, mine(p)).start()
+
+        @pl.when(p == q)
+        def _():
+            come[p] = out[p]
+
+    def head_local_theirs(i):
+        for u in range(GROUP):
+            head_local_one(theirs(target(i, u)))
+        for u in range(GROUP):
+            h = theirs(target(i, u))
+            remote(l_out.at[h], l_sib.at[h], lp_send, lp_recv.at[h], f, sib).start()
+
+    def head_local_mine(i):
+        for u in range(GROUP):
+            head_local_one(mine(target(i, u)))
+        for u in range(GROUP):
+            p = target(i, u)
+            h = mine(p)
+            arrived(l_sib.at[h], lp_recv.at[h])
+            own, other = l_out[h].astype(F32), l_sib[h].astype(F32)
+            joined = late_s[pl.ds(h, 1), :] * by_core(own, other) + by_core(other, own)
+            l_pair[p] = joined.astype(BF16)
+            hand_over(p, l_pair, l_in, l_send, l_recv)
+
+    def head_local_one(h):
         v = val[:, lanes(h)]
         mixing = (ws[h] * scores).astype(BF16)
         coef = (map_bt * we_s[pl.ds(h, 1), :]).astype(BF16)
@@ -217,56 +279,87 @@
         bs[h] = bs[h] + both[:T]
         l_out[h] = both[T:].astype(BF16)
 
-        @pl.when(h != k)
-        def _():
-            remote(l_out.at[h], l_in.at[k], l_send, l_recv.at[k], f, h).start()
-
-        @pl.when(h == k)
-        def _():
-            l_in[h] = l_out[h]
-
-    loop(heads + 1, head_local, 1)
+    loop(pairs // GROUP, head_local_theirs)
+    loop(pairs // GROUP, head_local_mine)
     loop(shards, h_away)
 
     def carry_wait(j):
-        g = ring(k, j, blocks)
+        g = ring(q, j, pairs)
         arrived(carry_in.at[g], k_recv.at[g])
 
-    loop(blocks, carry_wait, 1)
+    loop(pairs, carry_wait, 1)
 
     def chain(came, out, back, in_sem, send_sem, back_sem, backward):
         def link(i, state):
-            b = blocks - 1 - i if backward else i
+            b = pairs - 1 - i if backward else i
             out[b] = state.astype(BF16)
 
-            @pl.when(b != k)
+            @pl.when(b != q)
             def _():
                 arrived(came.at[b], in_sem.at[b])
 
             return carry_in[b, 0:1, :] * state + came[b].astype(F32)
 
-        lax.fori_loop(0, blocks, link, jnp.zeros((N, T), F32))
+        lax.fori_loop(0, pairs, link, jnp.zeros((N, T), F32))
 
         def give(j):
-            b = ring(k, j, blocks)
-            remote(out.at[b], back.at[k], send_sem, back_sem.at[k], f, b).start()
-
-        loop(blocks, give, 1)
-        back[k] = out[k]
-
-    chain(l_in, s_out, s_in, l_recv, s_send, s_recv, False)
+            b = ring(q, j, pairs)
+            remote(out.at[b], back.at[k], send_sem, back_sem.at[k], f, mine(b)).start()
+
+        loop(pairs, give, 1)
+        back[k] = out[q]
+
+    chain(l_in, s_out, s_raw, l_recv, s_send, s_recv, False)
 
     sg[...] = jnp.zeros_like(sg)
     acc_c[...] = jnp.zeros_like(acc_c)
     acc_b[...] = jnp.zeros_like(acc_b)
 
-    def head_error(j):
-        h = ring(k, heads - j, heads)
-
+    def await_head(h, back, sem):
         @pl.when(h != k)
         def _():
-            arrived(s_in.at[h], s_recv.at[h])
-
+            arrived(back.at[h], sem.at[h])
+
+    def error_group(hs):
+        parts = [head_error_one(h) for h in hs]
+        sg[...] += sum(p[0] for p in parts)
+        acc_c[...] += sum(p[1] for p in parts)
+
+    def entries(i):
+        for u in range(GROUP):
+            p = origin(i, u)
+            h = mine(p)
+            arrived(e_sib.at[h], ep_recv.at[h])
+            own, other = e_out[h].astype(F32), e_sib[h].astype(F32)
+            joined = by_core(own, other) + early_s[pl.ds(h, 1), :] * by_core(other, own)
+            e_pair[p] = joined.astype(BF16)
+            hand_over(p, e_pair, e_in, e_send, e_recv)
+
+    def head_error(i):
+        hs = [mine(origin(i, u)) for u in range(GROUP)]
+        for h in hs:
+            await_head(h, s_raw, s_recv)
+        for h in hs:
+            state = s_raw[h].astype(F32)
+            first_local = by_core(l_out[h], l_sib[h]).astype(F32)
+            after = early_s[pl.ds(h, 1), :] * state + first_local
+            s_in[h] = by_core(state, after).astype(BF16)
+            s_pass[h] = by_core(after, state).astype(BF16)
+            remote(s_pass.at[h], s_in.at[h], sp_send, sp_recv.at[h], f, sib).start()
+        error_group(hs)
+
+        @pl.when(i > 0)
+        def _():
+            entries(i - 1)
+
+        hs = [theirs(origin(i, u)) for u in range(GROUP)]
+        for h in hs:
+            arrived(s_in.at[h], sp_recv.at[h])
+        error_group(hs)
+        for h in hs:
+            remote(e_out.at[h], e_sib.at[h], ep_send, ep_recv.at[h], f, sib).start()
+
+    def head_error_one(h):
         v = val[:, lanes(h)]
         state = s_in[h]
         col = dcb[h]
@@ -277,22 +370,14 @@
         loss_s[pl.ds(h, 1), :] = jnp.sum(err * err, axis=0, keepdims=True)
         skip_s[pl.ds(h, 1), :] = jnp.sum(grad * v.astype(F32), axis=0, keepdims=True)
         mix_grad = ws[h] * dot_last(grad.astype(BF16), v)
-        sg[...] += mix_grad
         turn = mix_grad * scores * (col - decay_s[pl.ds(h, 1), :]) + grad * grown_state * col
         alog_s[pl.ds(h, 1), :] = jnp.sum(turn, axis=0, keepdims=True)
         grown = (growth * grad).astype(BF16)
         e_out[h] = dot(map_c_t, grown).astype(BF16)
-        acc_c[...] += dot_last(state, grown)
-
-        @pl.when(h != k)
-        def _():
-            remote(e_out.at[h], e_in.at[k], e_send, e_recv.at[k], f, h).start()
-
-        @pl.when(h == k)
-        def _():
-            e_in[h] = e_out[h]
-
-    loop(heads + 1, head_error, 1)
+        return mix_grad, dot_last(state, grown)
+
+    loop(pairs // GROUP, head_error)
+    entries(pairs // GROUP - 1)
 
     for hop in range(1, chips):
         j = ring(x, hop, chips) * 2 + c
@@ -300,24 +385,35 @@
         arrived(piece, h_recv.at[j])
         remote(piece, piece, h_fwd, h_recv.at[j], f, sib).start()
 
-    chain(e_in, x_out, x_in, e_recv, x_send, x_recv, True)
-
-    def head_exit(j):
-        h = ring(k, heads - j, heads)
-
-        @pl.when(h != k)
-        def _():
-            arrived(x_in.at[h], x_recv.at[h])
-
+    chain(e_in, x_out, x_raw, e_recv, x_send, x_recv, True)
+
+    def head_exit(i):
+        hs = [mine(origin(i, u)) for u in range(GROUP)]
+        for h in hs:
+            await_head(h, x_raw, x_recv)
+        for h in hs:
+            exit_late = x_raw[h].astype(F32)
+            entry_late = by_core(e_sib[h], e_out[h]).astype(F32)
+            exit_early = entry_late + late_s[pl.ds(h, 1), :] * exit_late
+            x_in[h] = by_core(exit_early, exit_late).astype(BF16)
+            x_pass[h] = by_core(exit_late, exit_early).astype(BF16)
+            remote(x_pass.at[h], x_in.at[h], xp_send, xp_recv.at[h], f, sib).start()
+        acc_b[...] += sum(head_exit_one(h) for h in hs)
+        hs = [theirs(origin(i, u)) for u in range(GROUP)]
+        for h in hs:
+            arrived(x_in.at[h], xp_recv.at[h])
+        acc_b[...] += sum(head_exit_one(h) for h in hs)
+
+    def head_exit_one(h):
         leaving = x_in[h]
         last = fin_s[pl.ds(h, 1), :]
         weighed = dot_last(leaving, val[:, lanes(h)]) * we_s[pl.ds(h, 1), :]
-        acc_b[...] += weighed
         end = jnp.sum(weighed * map_bt, axis=0, keepdims=True)
         kept = jnp.sum(leaving.astype(F32) * s_in[h].astype(F32), axis=0, keepdims=True)
         alog_s[pl.ds(h, 1), :] += end * (last - decay_s[pl.ds(h, 1), :]) + last * jnp.exp(last) * kept
-
-    loop(heads + 1, head_exit, 1)
+        return weighed
+
+    loop(pairs // GROUP, head_exit)
 
     score_bf = sg[...].astype(BF16)
     pg_out[0] = (dot(map_c_t, score_bf) + acc_b[...]).astype(BF16)
@@ -333,11 +429,13 @@
     loop(octet, pg_go, 1)
     pg_in[:, own_cols] = pg_out[c]
 
-    lane = lax.broadcasted_iota(jnp.int32, (heads, T), 1)
     alog = jnp.sum(alog_s[...], axis=1, keepdims=True)
     skip = jnp.sum(skip_s[...], axis=1, keepdims=True)
     loss = jnp.sum(loss_s[...], axis=1, keepdims=True) * (0.5 * scale)
-    c_out[...] = jnp.where(lane == 0, alog, jnp.where(lane == 1, skip, jnp.where(lane == 2, loss, 0.0)))
+    lane = lax.broadcasted_iota(jnp.int32, (heads, T), 1)
+    tile = jnp.where(lane == 0, alog, jnp.where(lane == 1, skip, jnp.where(lane == 2, loss, 0.0)))
+    square = jnp.concatenate([tile, jnp.zeros((T - heads, T), F32)], axis=0)
+    c_out[...] = jnp.transpose(square)[0:8]
 
     def c_go(j):
         remote(c_out, c_in.at[f], c_send, c_recv.at[f], ring(f, j, shards), k).start()
@@ -377,41 +475,58 @@
         arrived(c_in.at[g], c_recv.at[g])
 
     loop(shards, r_wait, 1)
-    y_out[0:N, :] = lax.fori_loop(0, shards, lambda i, s: s + r_in[i].astype(F32), jnp.zeros((N, T), F32))
-    y_out[N:, :] = lax.fori_loop(0, shards, lambda i, s: s + c_in[i], jnp.zeros((heads, T), F32))
+    total = r_in[0].astype(F32)
+    sums = c_in[0]
+    for i in range(1, shards):
+        total = total + r_in[i].astype(F32)
+        sums = sums + c_in[i]
+    y_out[...] = total.astype(BF16)
+    d_out[...] = sums
 
     for hop in range(1, rows):
-        remote(y_out, y_in.at[yh], y_send.at[hop], y_recv.at[yh], f, ring(yh, hop, rows) * octet + o).start()
+        there = ring(yh, hop, rows) * octet + o
+        remote(y_out, y_in.at[yh], y_send.at[hop], y_recv.at[yh], f, there).start()
+        remote(d_out, d_in.at[yh], d_send.at[hop], d_recv.at[yh], f, there).start()
     y_in[yh] = y_out[...]
+    d_in[yh] = d_out[...]
     for hop in range(1, rows):
         src = ring(yh, hop, rows)
         arrived(y_in.at[src], y_recv.at[src])
-    total = y_in[0]
+        arrived(d_in.at[src], d_recv.at[src])
+    total = y_in[0].astype(F32)
+    sums = d_in[0]
     for i in range(1, rows):
-        total = total + y_in[i]
-    z_out[...] = total
+        total = total + y_in[i].astype(F32)
+        sums = sums + d_in[i]
+    z_out[...] = total.astype(BF16)
+    t_out[...] = sums
 
     def z_go(j):
-        remote(z_out, z_in.at[o], z_send, z_recv.at[o], f, first + ring(o, j, octet)).start()
+        there = first + ring(o, j, octet)
+        remote(z_out, z_in.at[o], z_send, z_recv.at[o], f, there).start()
+        remote(t_out, t_in.at[o], t_send, t_recv.at[o], f, there).start()
 
     loop(octet, z_go, 1)
     z_in[o] = z_out[...]
+    t_in[o] = t_out[...]
 
     def z_wait(j):
         src = ring(o, j, octet)
         arrived(z_in.at[src], z_recv.at[src])
+        arrived(t_in.at[src], t_recv.at[src])
 
     loop(octet, z_wait, 1)
     for i in range(chips):
         ow[i * T : (i + 1) * T, :] = jnp.transpose(
-            jnp.concatenate([z_in[2 * i, 0:N, :], z_in[2 * i + 1, 0:N, :]], axis=0)
+            jnp.concatenate([z_in[2 * i], z_in[2 * i + 1]], axis=0).astype(F32)
         )
-    sums = z_in[0, N:, :]
+    sums = t_in[0]
     for i in range(1, octet):
-        sums = sums + z_in[i, N:, :]
+        sums = sums + t_in[i]
     osc[...] = sums
 
-    others = pl.ds(0, blocks - 1)
+    others = pl.ds(0, pairs - 1)
+    every = pl.ds(0, pairs)
     peers = pl.ds(0, shards - 1)
     left(wbuf.at[peers, pl.ds(0, part)], w_send)
     left(wbuf.at[:, pl.ds(0, (chips - 1) * part)], v_send)
@@ -422,16 +537,23 @@
     left(hq.at[pl.ds(0, T)], h_own)
     left(hq.at[pl.ds(0, (chips - 1) * T)], h_fwd)
     left(carry_out.at[others], k_send)
-    left(l_out.at[others], l_send)
+    left(fin_s, n_send)
+    left(l_pair.at[others], l_send)
     left(s_out.at[others], s_send)
-    left(e_out.at[others], e_send)
+    left(e_pair.at[others], e_send)
     left(x_out.at[others], x_send)
+    left(l_out.at[every], lp_send)
+    left(s_pass.at[every], sp_send)
+    left(e_out.at[every], ep_send)
+    left(x_pass.at[every], xp_send)
     left(pg_in.at[:, pl.ds(0, (octet - 1) * T)], p_send)
     left(r_out.at[peers], r_send)
     left(c_in.at[peers], c_send)
     for hop in range(1, rows):
         left(y_out, y_send.at[hop])
+        left(d_out, d_send.at[hop])
     left(z_in.at[pl.ds(0, octet - 1)], z_send)
+    left(t_in.at[pl.ds(0, octet - 1)], t_send)
 
 
 def local(hidden, values, targets, dt_raw, proj_weight, a_log, skip):
@@ -454,24 +576,27 @@
         vmem((octet * T, shards * T), BF16),
         vmem((heads, T, T), F32), vmem((heads, T, T), F32), vmem((heads, T, T), F32),
         *[small] * 8,
-        vmem((heads, 8, T), F32), vmem((blocks, 8, T), F32),
-        *[per_head(BF16)] * 8,
+        small, small, small, vmem((blocks // 2, 8, T), F32), vmem((blocks // 2, 8, T), F32),
+        *[per_head(BF16)] * 10,
+        *[vmem((blocks // 2, N, T), BF16)] * 6,
         vmem((T, T), F32), vmem((N, T), F32), vmem((N, T), F32),
         vmem((2, N, T), BF16), vmem((N, octet * T), BF16),
         vmem((shards, N, T), BF16), vmem((shards, N, T), BF16),
-        small, vmem((shards, heads, T), F32),
-        vmem((N + heads, T), F32), vmem((rows, N + heads, T), F32),
-        vmem((N + heads, T), F32), vmem((octet, N + heads, T), F32),
-        one, many(shards), one, many(octet), one, one, one, one, one, many(octet), one, many(blocks),
-        *[one, many(blocks)] * 4,
+        vmem((8, T), F32), vmem((shards, 8, T), F32),
+        vmem((N, T), BF16), vmem((rows, N, T), BF16),
+        vmem((N, T), BF16), vmem((octet, N, T), BF16),
+        vmem((8, T), F32), vmem((rows, 8, T), F32), vmem((8, T), F32), vmem((octet, 8, T), F32),
+        one, many(shards), one, many(octet), one, one, one, one, one, many(octet), one, one, one, many(blocks),
+        *[one, many(blocks)] * 8,
         one, many(octet), one, many(shards), one, many(shards), many(rows), many(rows), one, many(octet),
+        many(rows), many(rows), one, many(octet),
     ]
     spec = pl.BlockSpec(memory_space=vmem)
     grad_w, sums = pl.pallas_call(
         functools.partial(body, shards, blocks, scale),
         out_shape=(
             jax.ShapeDtypeStruct((wide, both), F32),
-            jax.ShapeDtypeStruct((heads, T), F32),
+            jax.ShapeDtypeStruct((8, T), F32),
         ),
         in_specs=[pl.BlockSpec(memory_space=pltpu.HBM)] * 5 + [pl.BlockSpec(memory_space=pltpu.SMEM)] * 2,
         out_specs=(spec, spec),
@@ -480,7 +605,7 @@
             collective_id=0, has_side_effects=True, vmem_limit_bytes=56 * 2**20
         ),
     )(hidden[0], values[0], targets[0], dt_raw[0], proj_weight, a_log, skip)
-    return (grad_w, sums[:, 0], sums[:, 1], jnp.sum(sums[:, 2]))
+    return (grad_w, sums[0, :heads], sums[1, :heads], jnp.sum(sums[2, :heads]))
 
 
 def solution(mesh):

time: 143 us -> 122 us (0.85)
  Pallas kernels: 139 us -> 118 us
    pallas_call x1, Pallas kernels: 139 us -> 118 us  [local(): pl.pallas_call(functools.partial(body, shards, blocks, scale), out_shape=...]
where the time goes in v3:
time: 122 us
  Pallas kernels  118 us (97%)
  other arithmetic  1.9 us (2%)
  local copies, waits for them, and re-layouts  1.67 us (1%)
    pallas_call x1, Pallas kernels, local(): pl.pallas_call(functools.partial(body, shards, blocks, scale), out_shape=...  118 us

profile of v3, /device:TPU:1, one launch (start us, length us, event | category | flops | bytes accessed | tf_op | source)
XLA Modules:
  0.0 122.0 jit_solution(10725421135155142981)
XLA Ops:
  0.6 117.8 %shard_map.102 = (f32[512,128]{1,0:T(8,128)}, f32[8,128]{1,0:T(8,128)}) custom-call(bf16[128,8192]{1,0:T(8,128)(2,1)} %bitcast.8, bf16[128,4096]{1,0:T(8,128)(2,1)} %bitcast.9, bf16[128,4096]{1,0:T(8,128)(2,1)} %bitcast.10, f32[32,128]{1,0:T(8,128)} %bitcast.11, bf16[512,128]{1,0:T(8,128)(2,1)} %w_h.1, f32[32]{0:T(128)} %a_ref.1, f32[32]{0:T(128)} %skip_ref.1), custom_call_target="tpu_custom_call" | custom-call | tf_op jit(solution)/shard_map/pallas_call | solution.py:595
  118.4 1.9 %slice_reduce_fusion = (f32[]{:T(128)}, f32[32]{0:T(128)}, f32[32]{0:T(128)}) fusion(f32[8,128]{1,0:T(8,128)} %get-tuple-element.7), kind=kLoop, calls=%fused_computation | loop fusion | flops 31 | bytes 644 | tf_op jit(solution)/shard_map/reduce_sum | solution.py:608
  120.3 1.7 %copy.12 = f32[512,128]{1,0:T(8,128)} copy(f32[512,128]{1,0:T(8,128)} %get-tuple-element.15) | data formatting | bytes 524288

commit v4 on v3

--- a/solution.py
+++ b/solution.py
@@ -29,19 +29,19 @@
 def body(
     shards, blocks, scale,
     hid_h, val_h, tgt_h, dt_h, w_h, a_ref, skip_ref, ow, osc,
-    hid, val, tgt, dt, w, in_sem, wbuf, hq, ws, dcb, bs, rate_s, step_s, decay_s, fin_s, we_s, alog_s, skip_s, loss_s,
+    hid, val, tgt, dt, in_sem, wbuf, hq, ws, dcb, bs, rate_s, step_s, decay_s, fin_s, we_s, alog_s, skip_s, loss_s,
     fin_sib, early_s, late_s, carry_out, carry_in,
     l_out, l_sib, s_raw, s_pass, s_in, e_out, e_sib, x_raw, x_pass, x_in,
     l_pair, l_in, s_out, e_pair, e_in, x_out,
     sg, acc_c, acc_b, pg_out, pg_in, r_out, r_in, c_out, c_in, y_out, y_in, z_out, z_in, d_out, d_in, t_out, t_in,
-    w_send, w_recv, v_send, v_recv, u_send, h_send, h_far, h_own, h_fwd, h_recv, n_send, n_recv, k_send, k_recv,
+    w_send, w_recv, v_send, v_recv, u_send, h_send, h_fwd, h_recv, n_send, n_recv, k_send, k_recv,
     l_send, l_recv, s_send, s_recv, e_send, e_recv, x_send, x_recv,
     lp_send, lp_recv, sp_send, sp_recv, ep_send, ep_recv, xp_send, xp_recv,
     p_send, p_recv, r_send, r_recv, c_send, c_recv, y_send, y_recv, z_send, z_recv,
     d_send, d_recv, t_send, t_recv,
 ):
     heads = dt.shape[0]
-    wide = w.shape[0]
+    wide = w_h.shape[0]
     part = wide // (2 * ROW_CHIPS)
     chips = ROW_CHIPS
     octet = 2 * chips
@@ -104,22 +104,22 @@
     loop(blocks, greet_k, 1)
     loads = [
         pltpu.make_async_copy(src, dst, in_sem.at[i])
-        for i, (src, dst) in enumerate(((w_h, w), (dt_h, dt), (val_h, val), (tgt_h, tgt), (hid_h, hid)))
+        for i, (src, dst) in enumerate(((dt_h, dt), (val_h, val), (tgt_h, tgt), (hid_h, hid)), 1)
     ]
     for load in loads:
         load.start()
+    pl.semaphore_wait(barrier, shards + blocks - 2)
+
+    own_part = pl.ds(pl.multiple_of(o * part, part), part)
+
+    def w_go(j):
+        remote(w_h.at[own_part], wbuf.at[f, own_part], w_send, w_recv.at[f], ring(f, j, shards), k).start()
+
+    loop(shards, w_go, 1)
+    own_copy = pltpu.make_async_copy(w_h.at[own_part], wbuf.at[f, own_part], in_sem.at[0])
+    own_copy.start()
+
     loads[0].wait()
-    pl.semaphore_wait(barrier, shards + blocks - 2)
-
-    own_part = pl.ds(pl.multiple_of(o * part, part), part)
-
-    def w_go(j):
-        remote(w.at[own_part], wbuf.at[f, own_part], w_send, w_recv.at[f], ring(f, j, shards), k).start()
-
-    loop(shards, w_go, 1)
-    wbuf[f, own_part, :] = w[own_part, :]
-
-    loads[1].wait()
 
     def spread(h):
         rate_s[pl.ds(h, 1), :] = jnp.full((1, T), a_ref[h], F32)
@@ -150,6 +150,7 @@
             there = first + ring(x, hop, chips) * 2 + c
             remote(slot, slot, v_send, v_recv.at[o], f, there).start()
 
+    own_copy.wait()
     loop(shards, w_pass)
     own_slab = wbuf.at[:, own_part]
     remote(own_slab, own_slab, u_send, v_recv.at[o], f, sib).start()
@@ -175,30 +176,42 @@
 
     own_rows = pl.ds(pl.multiple_of(o * T, T), T)
 
-    def hid_to(i, hop, sem):
-        there = ring(x, hop, chips)
-        remote(
-            hid.at[:, pl.ds(pl.multiple_of(i * wide + there * T, T), T)], hq.at[own_rows, lanes(i)],
-            sem, h_recv.at[o], f, first + there * 2 + c,
-        ).start()
-
-    loads[4].wait()
-
-    def h_near(i):
-        hid_to(i, 1, h_send)
-        if chips > 2:
-            hid_to(i, chips - 1, h_send)
+    near_end, mid_end = shards * 3 // 8, shards * 3 // 4
+
+    def h_go(i):
+        part = jnp.where(i < mid_end, 0, octet)
+        for hop in range(1, chips):
+            there = ring(x, hop, chips)
+            remote(
+                hid.at[:, pl.ds(pl.multiple_of(i * wide + there * T, T), T)], hq.at[own_rows, lanes(i)],
+                h_send, h_recv.at[part + o], f, first + there * 2 + c,
+            ).start()
+
+    def h_keep(i):
         hq[own_rows, lanes(i)] = hid[:, pl.ds(pl.multiple_of(i * wide + x * T, T), T)]
 
-    def h_away(i):
-        for hop in range(2, chips - 1):
-            hid_to(i, hop, h_far)
-
-    loop(shards, h_near)
-    remote(hq.at[own_rows], hq.at[own_rows], h_own, h_recv.at[o], f, sib).start()
-
+    def h_slab(src, late):
+        start, size = (mid_end, shards - mid_end) if late else (0, mid_end)
+        return hq.at[pl.ds(pl.multiple_of(src * T, T), T), pl.ds(start * T, size * T)]
+
+    def h_next(src, late):
+        there = h_recv.at[src + (octet if late else 0)]
+        remote(h_slab(src, late), h_slab(src, late), h_fwd, there, f, sib).start()
+
+    def h_pass(late):
+        for hop in range(1, chips):
+            src = ring(x, hop, chips) * 2 + c
+            arrived(h_slab(src, late), h_recv.at[src + (octet if late else 0)])
+            h_next(src, late)
+
+    loads[3].wait()
+    loop(near_end, h_go)
+    loop(shards, h_keep)
+    h_next(o, False)
+    h_next(o, True)
+
+    loads[1].wait()
     loads[2].wait()
-    loads[3].wait()
     lower = row_id >= col_id
 
     def head_start(i):
@@ -281,7 +294,6 @@
 
     loop(pairs // GROUP, head_local_theirs)
     loop(pairs // GROUP, head_local_mine)
-    loop(shards, h_away)
 
     def carry_wait(j):
         g = ring(q, j, pairs)
@@ -310,6 +322,7 @@
         back[k] = out[q]
 
     chain(l_in, s_out, s_raw, l_recv, s_send, s_recv, False)
+    loop(mid_end, h_go, near_end)
 
     sg[...] = jnp.zeros_like(sg)
     acc_c[...] = jnp.zeros_like(acc_c)
@@ -379,13 +392,10 @@
     loop(pairs // GROUP, head_error)
     entries(pairs // GROUP - 1)
 
-    for hop in range(1, chips):
-        j = ring(x, hop, chips) * 2 + c
-        piece = hq.at[pl.ds(pl.multiple_of(j * T, T), T)]
-        arrived(piece, h_recv.at[j])
-        remote(piece, piece, h_fwd, h_recv.at[j], f, sib).start()
+    h_pass(False)
 
     chain(e_in, x_out, x_raw, e_recv, x_send, x_recv, True)
+    loop(shards, h_go, mid_end)
 
     def head_exit(i):
         hs = [mine(origin(i, u)) for u in range(GROUP)]
@@ -443,9 +453,12 @@
     loop(shards, c_go, 1)
     c_in[f] = c_out[...]
 
+    h_pass(True)
+
     def h_wait(j):
         src = j * 2 + 1 - c
-        arrived(hq.at[pl.ds(pl.multiple_of(src * T, T), T)], h_recv.at[src])
+        arrived(h_slab(src, False), h_recv.at[src])
+        arrived(h_slab(src, True), h_recv.at[octet + src])
 
     loop(chips, h_wait)
 
@@ -456,18 +469,21 @@
     loop(octet, pg_wait, 1)
 
     def r_go(j):
-        g = ring(f, j, shards)
-        r_out[g] = dot(pg_in[...], hq[:, lanes(g)]).astype(BF16)
-
-        @pl.when(g != f)
-        def _():
-            remote(r_out.at[g], r_in.at[f], r_send, r_recv.at[f], g, k).start()
-
-        @pl.when(g == f)
-        def _():
-            r_in[g] = r_out[g]
-
-    loop(shards + 1, r_go, 1)
+        two = ring(lax.div(f, 2), j, shards // 2)
+        product = dot(pg_in[...], hq[:, pl.ds(pl.multiple_of(two * 2 * T, 2 * T), 2 * T)]).astype(BF16)
+        for u in range(2):
+            g = two * 2 + u
+            r_out[g] = product[:, u * T : (u + 1) * T]
+
+            @pl.when(g != f)
+            def _():
+                remote(r_out.at[g], r_in.at[f], r_send, r_recv.at[f], g, k).start()
+
+            @pl.when(g == f)
+            def _():
+                r_in[g] = r_out[g]
+
+    loop(shards // 2 + 1, r_go, 1)
 
     def r_wait(j):
         g = ring(f, j, shards)
@@ -531,11 +547,8 @@
     left(wbuf.at[peers, pl.ds(0, part)], w_send)
     left(wbuf.at[:, pl.ds(0, (chips - 1) * part)], v_send)
     left(wbuf.at[:, pl.ds(0, chips * part)], u_send)
-    left(hq.at[pl.ds(0, min(2, chips - 1) * T)], h_send)
-    if chips > 3:
-        left(hq.at[pl.ds(0, (chips - 3) * T)], h_far)
-    left(hq.at[pl.ds(0, T)], h_own)
-    left(hq.at[pl.ds(0, (chips - 1) * T)], h_fwd)
+    left(hq.at[pl.ds(0, (chips - 1) * T)], h_send)
+    left(hq.at[pl.ds(0, chips * T)], h_fwd)
     left(carry_out.at[others], k_send)
     left(fin_s, n_send)
     left(l_pair.at[others], l_send)
@@ -571,7 +584,7 @@
     many = lambda n: pltpu.SemaphoreType.DMA((n,))
     scratch = [
         vmem(hidden.shape[1:], BF16), vmem(values.shape[1:], BF16), vmem(targets.shape[1:], BF16),
-        small, vmem((wide, both), BF16), many(5),
+        small, many(5),
         vmem((shards, wide, both), BF16),
         vmem((octet * T, shards * T), BF16),
         vmem((heads, T, T), F32), vmem((heads, T, T), F32), vmem((heads, T, T), F32),
@@ -586,7 +599,7 @@
         vmem((N, T), BF16), vmem((rows, N, T), BF16),
         vmem((N, T), BF16), vmem((octet, N, T), BF16),
         vmem((8, T), F32), vmem((rows, 8, T), F32), vmem((8, T), F32), vmem((octet, 8, T), F32),
-        one, many(shards), one, many(octet), one, one, one, one, one, many(octet), one, one, one, many(blocks),
+        one, many(shards), one, many(octet), one, one, one, many(2 * octet), one, one, one, many(blocks),
         *[one, many(blocks)] * 8,
         one, many(octet), one, many(shards), one, many(shards), many(rows), many(rows), one, many(octet),
         many(rows), many(rows), one, many(octet),

time: 122 us -> 117 us (0.959)
  Pallas kernels: 118 us -> 112 us
    pallas_call x1, Pallas kernels: 118 us -> 112 us  [local(): pl.pallas_call(functools.partial(body, shards, blocks, scale), out_shape=...]
where the time goes in v4:
time: 117 us
  Pallas kernels  112 us (96%)
  other arithmetic  1.9 us (2%)
  local copies, waits for them, and re-layouts  1.67 us (1%)
    pallas_call x1, Pallas kernels, local(): pl.pallas_call(functools.partial(body, shards, blocks, scale), out_shape=...  112 us

profile of v4, /device:TPU:1, one launch (start us, length us, event | category | flops | bytes accessed | tf_op | source)
XLA Modules:
  0.0 116.6 jit_solution(3283560026800035802)
XLA Ops:
  0.6 112.3 %shard_map.102 = (f32[512,128]{1,0:T(8,128)}, f32[8,128]{1,0:T(8,128)}) custom-call(bf16[128,8192]{1,0:T(8,128)(2,1)} %bitcast.8, bf16[128,4096]{1,0:T(8,128)(2,1)} %bitcast.9, bf16[128,4096]{1,0:T(8,128)(2,1)} %bitcast.10, f32[32,128]{1,0:T(8,128)} %bitcast.11, bf16[512,128]{1,0:T(8,128)(2,1)} %w_h.1, f32[32]{0:T(128)} %a_ref.1, f32[32]{0:T(128)} %skip_ref.1), custom_call_target="tpu_custom_call" | custom-call | tf_op jit(solution)/shard_map/pallas_call | solution.py:608
  113.0 1.9 %slice_reduce_fusion = (f32[]{:T(128)}, f32[32]{0:T(128)}, f32[32]{0:T(128)}) fusion(f32[8,128]{1,0:T(8,128)} %get-tuple-element.7), kind=kLoop, calls=%fused_computation | loop fusion | flops 31 | bytes 644 | tf_op jit(solution)/shard_map/reduce_sum | solution.py:621
  114.9 1.7 %copy.12 = f32[512,128]{1,0:T(8,128)} copy(f32[512,128]{1,0:T(8,128)} %get-tuple-element.15) | data formatting | bytes 524288

commit v5 on v4

--- a/solution.py
+++ b/solution.py
@@ -98,17 +98,21 @@
         pl.semaphore_signal(barrier, inc=1, device_id=(ring(f, j, shards), k), device_id_type=MESH)
 
     def greet_k(j):
-        pl.semaphore_signal(barrier, inc=1, device_id=(f, ring(k, j, blocks)), device_id_type=MESH)
+        pl.semaphore_signal(barrier, inc=1, device_id=(f, mine(ring(q, j, pairs))), device_id_type=MESH)
+
+    def greet_run(j):
+        pl.semaphore_signal(barrier, inc=1, device_id=(f, first + theirs(j)), device_id_type=MESH)
 
     loop(shards, greet_f, 1)
-    loop(blocks, greet_k, 1)
+    loop(pairs, greet_k, 1)
+    loop(chips, greet_run)
     loads = [
         pltpu.make_async_copy(src, dst, in_sem.at[i])
         for i, (src, dst) in enumerate(((dt_h, dt), (val_h, val), (tgt_h, tgt), (hid_h, hid)), 1)
     ]
     for load in loads:
         load.start()
-    pl.semaphore_wait(barrier, shards + blocks - 2)
+    pl.semaphore_wait(barrier, shards + pairs + chips - 2)
 
     own_part = pl.ds(pl.multiple_of(o * part, part), part)
 

time: 117 us -> 115 us (0.983)
    pallas_call x1, Pallas kernels: 112 us -> 111 us  [local(): pl.pallas_call(functools.partial(body, shards, blocks, scale), out_shape=...]
where the time goes in v5:
time: 115 us
  Pallas kernels  111 us (97%)
  other arithmetic  1.9 us (2%)
  local copies, waits for them, and re-layouts  1.67 us (1%)
    pallas_call x1, Pallas kernels, local(): pl.pallas_call(functools.partial(body, shards, blocks, scale), out_shape=...  111 us

profile of v5, /device:TPU:1, one launch (start us, length us, event | category | flops | bytes accessed | tf_op | source)
XLA Modules:
  0.0 114.9 jit_solution(4481578372964064332)
XLA Ops:
  0.6 110.7 %shard_map.102 = (f32[512,128]{1,0:T(8,128)}, f32[8,128]{1,0:T(8,128)}) custom-call(bf16[128,8192]{1,0:T(8,128)(2,1)} %bitcast.8, bf16[128,4096]{1,0:T(8,128)(2,1)} %bitcast.9, bf16[128,4096]{1,0:T(8,128)(2,1)} %bitcast.10, f32[32,128]{1,0:T(8,128)} %bitcast.11, bf16[512,128]{1,0:T(8,128)(2,1)} %w_h.1, f32[32]{0:T(128)} %a_ref.1, f32[32]{0:T(128)} %skip_ref.1), custom_call_target="tpu_custom_call" | custom-call | tf_op jit(solution)/shard_map/pallas_call | solution.py:612
  111.3 1.9 %slice_reduce_fusion = (f32[]{:T(128)}, f32[32]{0:T(128)}, f32[32]{0:T(128)}) fusion(f32[8,128]{1,0:T(8,128)} %get-tuple-element.7), kind=kLoop, calls=%fused_computation | loop fusion | flops 31 | bytes 644 | tf_op jit(solution)/shard_map/reduce_sum | solution.py:625
  113.2 1.7 %copy.12 = f32[512,128]{1,0:T(8,128)} copy(f32[512,128]{1,0:T(8,128)} %get-tuple-element.15) | data formatting | bytes 524288
